TPU v7x, 256 devices: a whole 4x4x8 slice. The times are simulated.
256 devices in a mesh: gx: 16 (over z, core), gy: 16 (over y, x).
Axes of the slice: x: 4, y: 4, z: 8, core: 2. Of those that a mesh axis runs over, the one named last changes fastest.
Arguments:
- pressure: float32 [32, 512, 2048], P(None, 'gx', 'gy'), may hold values from -4 to 4
- ksat: float32 [32, 512, 2048], P(None, 'gx', 'gy'), may hold values from 0.2 to 2
- age_mean: float32 [32, 512, 2048], P(None, 'gx', 'gy'), may hold values from 1 to 10
- age_var: float32 [32, 512, 2048], P(None, 'gx', 'gy'), may hold values from 0.5 to 5
- remap: int32 [512, 16], P('gx', 'gy'), may hold values from 0 to 511, as said below
- forcing: float32 [7, 512, 2048], P(None, 'gx', 'gy'), may hold values from 0 to 1.5
- land_state: float32 [2, 512, 2048], P(None, 'gx', 'gy'), may hold values from 0 to 1
- veg_class: int32 [512, 2048], P('gx', 'gy'), may hold values from 0 to 16
- veg_table: float32 [5, 17], replicated, may hold values from 0.3 to 0.9
Outputs:
- pressure_next: float32 [32, 512, 2048], P(None, 'gx', 'gy')
- age_mean_next: float32 [32, 512, 2048], P(None, 'gx', 'gy')
- age_var_next: float32 [32, 512, 2048], P(None, 'gx', 'gy')
- land_next: float32 [2, 512, 2048], P(None, 'gx', 'gy')
Inputs may be any that keep to these rules, and one draw needn't show every extreme that they name: `remap`: each entry is d * 32 + s: the tile is handled by slot s of the device at index d along gy with the same gx index; within each gx index every slot receives exactly one tile. A device hands 0, 2 or 4 tiles to each device along gy, and in every draw some device hands 4 tiles to some device.
All inputs are finite; a program needn't handle non-finite values.
Results may differ from a plain program's by a relative error of at most 0.0003.
Values sent between devices are 32-bit elements; how exact they have to be, the bound alone decides.
A program may use at most 64 MiB of HBM per device.

v0:
```python
import jax
import jax.numpy as jnp
from jax import lax
from jax.sharding import PartitionSpec as P

NROOT = 2


step_time = 0.2
side_weight = 0.5


def padded(shard, sides, width):
    for axis, dim in sides:
        size, length = (lax.axis_size(axis), shard.shape[dim])
        up = [(i, (i + 1) % size) for i in range(size - 1)]
        down = [(j, i) for i, j in up]
        last = lax.slice_in_dim(shard, length - width, length, axis=dim)
        first = lax.slice_in_dim(shard, 0, width, axis=dim)
        before = lax.ppermute(last, axis, up)
        after = lax.ppermute(first, axis, down)
        shard = jnp.concatenate([before, shard, after], axis=dim)
    return shard


def water_content(head_field):
    return 0.05 + 0.4 * jax.nn.sigmoid(head_field)


def conductance(head_field, ksat_field):
    wetness = jax.nn.sigmoid(head_field)
    return ksat_field * (0.05 + wetness * wetness)


def vertical_net(vertical_q, template):
    zero_layer = jnp.zeros_like(template[:1])
    return jnp.concatenate([vertical_q, zero_layer], 0) - jnp.concatenate(
        [zero_layer, vertical_q], 0
    )


def layer_sources(sources, template):
    roots = sources.shape[0] - 1
    rest = jnp.zeros_like(template[roots:])
    extraction = jnp.concatenate([sources[1:], rest], 0)
    inflow = jnp.concatenate([sources[:1], jnp.zeros_like(template[1:])], 0)
    return (extraction, inflow)


def neighbour_parts():
    return [
        (slice(None, -2), slice(1, -1)),
        (slice(2, None), slice(1, -1)),
        (slice(1, -1), slice(None, -2)),
        (slice(1, -1), slice(2, None)),
    ]


def thomas(lower, diagonal, upper, right):
    layers = diagonal.shape[0]
    ratios = [upper[0] / diagonal[0]]
    values = [right[0] / diagonal[0]]
    for layer in range(1, layers):
        pivot = diagonal[layer] - lower[layer] * ratios[-1]
        ratios.append(upper[layer] / pivot)
        values.append((right[layer] - lower[layer] * values[-1]) / pivot)
    result = [values[-1]]
    for layer in range(layers - 2, -1, -1):
        result.append(values[layer] - ratios[layer] * result[-1])
    return jnp.stack(result[::-1], 0)


def newton_step(head_ext, ksat_ext, head_old, sources):
    centre = head_ext[:, 1:-1, 1:-1]
    conduct_all = conductance(head_ext, ksat_ext)
    conduct_mid = conduct_all[:, 1:-1, 1:-1]
    side_out = jnp.zeros_like(centre)
    side_diag = jnp.zeros_like(centre)
    for row_part, col_part in neighbour_parts():
        face_k = side_weight * jnp.sqrt(conduct_mid * conduct_all[:, row_part, col_part])
        side_out = side_out + face_k * (centre - head_ext[:, row_part, col_part])
        side_diag = side_diag + face_k
    vertical_k = jnp.sqrt(conduct_mid[:-1] * conduct_mid[1:])
    vertical_q = vertical_k * (centre[:-1] - centre[1:] + 1.0)
    extraction, inflow = layer_sources(sources, centre)
    residual = (
        (water_content(centre) - water_content(head_old)) / step_time
        + side_out
        + vertical_net(vertical_q, centre)
        + extraction
        - inflow
    )
    wetness = jax.nn.sigmoid(centre)
    zero_layer = jnp.zeros_like(centre[:1])
    k_below = jnp.concatenate([vertical_k, zero_layer], 0)
    k_above = jnp.concatenate([zero_layer, vertical_k], 0)
    diagonal = 0.4 * wetness * (1.0 - wetness) / step_time + side_diag + k_below + k_above
    update = thomas(-k_above, diagonal, -k_below, -residual)
    return centre + update


def age_step(head_ext, ksat_ext, age_ext, mom_ext, head_old, sources):
    centre = head_ext[:, 1:-1, 1:-1]
    conduct_all = conductance(head_ext, ksat_ext)
    conduct_mid = conduct_all[:, 1:-1, 1:-1]
    age_mid = age_ext[:, 1:-1, 1:-1]
    mom_mid = mom_ext[:, 1:-1, 1:-1]
    age_out = jnp.zeros_like(centre)
    mom_out = jnp.zeros_like(centre)
    for row_part, col_part in neighbour_parts():
        side_q = (
            side_weight
            * jnp.sqrt(conduct_mid * conduct_all[:, row_part, col_part])
            * (centre - head_ext[:, row_part, col_part])
        )
        flow_out = jnp.maximum(side_q, 0.0)
        flow_in = jnp.minimum(side_q, 0.0)
        age_out = age_out + flow_out * age_mid + flow_in * age_ext[:, row_part, col_part]
        mom_out = mom_out + flow_out * mom_mid + flow_in * mom_ext[:, row_part, col_part]
    vertical_k = jnp.sqrt(conduct_mid[:-1] * conduct_mid[1:])
    vertical_q = vertical_k * (centre[:-1] - centre[1:] + 1.0)
    down_plus = jnp.maximum(vertical_q, 0.0)
    down_minus = jnp.minimum(vertical_q, 0.0)
    age_down = down_plus * age_mid[:-1] + down_minus * age_mid[1:]
    mom_down = down_plus * mom_mid[:-1] + down_minus * mom_mid[1:]
    extraction, inflow = layer_sources(sources, centre)
    water_old = water_content(head_old)
    water_new = water_content(centre)
    age_next = (
        water_old * age_mid
        - step_time * (age_out + vertical_net(age_down, centre) + extraction * age_mid)
        + step_time * water_new
    ) / water_new
    mom_next = (
        water_old * mom_mid
        - step_time * (mom_out + vertical_net(mom_down, centre) + extraction * mom_mid)
        + 2.0 * step_time * water_new * age_next
    ) / water_new
    return (age_next, mom_next - age_next * age_next)


def land_step(land_top, forcing, land_state, veg_class, veg_table):
    veg_count = veg_table.shape[1]
    veg_params = jnp.zeros((veg_table.shape[0],) + veg_class.shape, forcing.dtype)
    for veg_id in range(veg_count):
        veg_params = (
            veg_params
            + jnp.where(veg_class == veg_id, 1.0, 0.0).astype(forcing.dtype)[None]
            * veg_table[:, veg_id][:, None, None]
        )
    albedo, conduct, capacity, et_factor, root_decay = (
        veg_params[0],
        veg_params[1],
        veg_params[2],
        veg_params[3],
        veg_params[4],
    )
    shortwave, longwave, air_temp, humidity = (forcing[0], forcing[1], forcing[2], forcing[3])
    wind_speed, surf_press, rainfall = (forcing[4], forcing[5], forcing[6])
    skin_temp, canopy = (land_state[0], land_state[1])
    roots = land_top.shape[0] - 1
    skin_next = (
        skin_temp + 0.5 * ((1.0 - albedo) * 2.0 * shortwave + 0.5 * longwave + air_temp)
    ) / 1.5
    demand = (
        conduct
        * jax.nn.softplus(skin_next)
        * (1.0 + wind_speed)
        * (1.0 - 0.5 * humidity)
        / (0.5 + surf_press)
    )
    root_scale = (1.0 - root_decay) / (1.0 - root_decay**roots)
    extracts = [
        0.5 * et_factor * demand * root_scale * root_decay**layer * jax.nn.sigmoid(land_top[layer])
        for layer in range(roots)
    ]
    wetted = canopy + rainfall
    dripping = jnp.maximum(wetted - capacity, 0.0)
    canopy_next = (wetted - dripping) * capacity / (demand + capacity)
    throughfall = dripping + 0.5 * rainfall
    infil_limit = land_top[roots] * (1.0 + 2.0 * (1.0 - jax.nn.sigmoid(land_top[0])))
    infiltration = infil_limit * throughfall / (infil_limit + throughfall)
    return (jnp.stack([infiltration] + extracts, 0), jnp.stack([skin_next, canopy_next], 0))


def pressure_rim(field):
    return padded(field, (("gx", 1), ("gy", 2)), 1)


def shards(pressure, ksat, age_mean, age_var, remap, forcing, land_state, veg_class, veg_table):
    top_fields = jnp.concatenate([pressure[:NROOT], ksat[:1]], 0)
    brick_rows = pressure.shape[1]
    row_groups = lax.axis_size("gy")
    tile_codes = remap[:, 0]
    highest = lax.Precision.HIGHEST
    gathered, all_codes = (
        lax.all_gather(top_fields, "gy", axis=1, tiled=True),
        lax.all_gather(remap, "gy", axis=0, tiled=True),
    )
    own_slots = jnp.arange(brick_rows, dtype=jnp.int32) + lax.axis_index("gy") * brick_rows
    picker = (all_codes[None, :, 0] == own_slots[:, None]).astype(jnp.float32)
    land_top = jnp.einsum("st,fty->fsy", picker, gathered, precision=highest)
    land_fluxes, land_next = land_step(land_top, forcing, land_state, veg_class, veg_table)
    all_fluxes = lax.all_gather(land_fluxes, "gy", axis=1, tiled=True)
    back_picker = (
        tile_codes[:, None] == jnp.arange(row_groups * brick_rows, dtype=jnp.int32)[None, :]
    ).astype(jnp.float32)
    soil_fluxes = jnp.einsum("xt,gty->gxy", back_picker, all_fluxes, precision=highest)
    moment = age_var + age_mean * age_mean
    fixed_rim = padded(jnp.stack([ksat, age_mean, moment], 0), (("gx", 2), ("gy", 3)), 1)
    ksat_ext = fixed_rim[0]
    current = pressure
    for newton_turn in range(2):
        current = newton_step(pressure_rim(current), ksat_ext, pressure, soil_fluxes)
    age_next, var_next = age_step(
        pressure_rim(current), ksat_ext, fixed_rim[1], fixed_rim[2], pressure, soil_fluxes
    )
    return (current, age_next, var_next, land_next)


def solution(mesh):
    return jax.shard_map(
        shards,
        mesh=mesh,
        in_specs=(
            P(None, "gx", "gy"),
            P(None, "gx", "gy"),
            P(None, "gx", "gy"),
            P(None, "gx", "gy"),
            P("gx", "gy"),
            P(None, "gx", "gy"),
            P(None, "gx", "gy"),
            P("gx", "gy"),
            P(),
        ),
        out_specs=(
            P(None, "gx", "gy"),
            P(None, "gx", "gy"),
            P(None, "gx", "gy"),
            P(None, "gx", "gy"),
        ),
        check_vma=False,
    )
```

profile of v0, /device:TPU:105, one launch (start us, length us, event | category | flops | bytes accessed | tf_op | source)
XLA Modules:
  0.0 192.3 jit_solution(16764964253635598068)
XLA Ops:
  0.7 1.4 add_bitcast_fusion
  2.2 0.7 pad_maximum_fusion.31
  2.8 5.3 %collective-permute-start = (f32[3,32,1,128]{3,2,1,0:T(1,128)}, f32[3,32,1,128]{3,2,1,0:T(1,128)S(1)}, u32[]{:S(2)}, u32[]{:S(2)}) collective-permute-start(f32[3,32,1,128]{3,2,1,0:T(1,128)} %get-tuple-element.162), channel_id=1, source_target_pairs={{0,16},{16,32},{32,48},{48,64},{64,80},{80,96},{96,112},{112,128},... | collective-permute-start | bytes 147464 | tf_op jit(solution)/shard_map/ppermute | solution.py:20
  8.2 1.9 collective-permute-start.1
  10.1 0.6 fusion.248
  10.7 4.8 %collective-permute-start.4 = (f32[32,1,128]{2,1,0:T(1,128)}, f32[32,1,128]{2,1,0:T(1,128)S(1)}, u32[]{:S(2)}, u32[]{:S(2)}) collective-permute-start(f32[32,1,128]{2,1,0:T(1,128)} %get-tuple-element.174), channel_id=1, source_target_pairs={{0,16},{16,32},{32,48},{48,64},{64,80},{80,96},{96,112},{112,128},... | collective-permute-start | bytes 49160 | tf_op jit(solution)/shard_map/ppermute | solution.py:20
  15.6 1.9 collective-permute-start.5
  17.6 1.0 slice_reduce_fusion.16
  18.6 0.6 dynamic-slice
  19.9 12.2 %all-reduce.14 = s32[512]{0:T(512)} all-reduce(s32[512]{0:T(512)S(1)} %bitcast_dynamic-update-slice_fusion), channel_id=1, replica_groups=mesh['gx'=16,'gy'=16] {'gy'}, use_global_device_ids=true, to_apply=%add.14 | all-reduce | flops 512 | bytes 4096
  32.3 18.4 %all_gather.9 = f32[3,512,128]{2,1,0:T(8,128)S(1)} all-gather(f32[3,32,128]{2,1,0:T(8,128)S(1)} %pad_maximum_fusion.32), channel_id=1, replica_groups=mesh['gx'=16,'gy'=16] {'gy'}, dimensions={1}, use_global_device_ids=true | all-gather | bytes 835584 | tf_op jit(solution)/shard_map/all_gather | solution.py:197
  50.8 1.1 convolution_bitcast_fusion.1
  52.2 1.4 add_divide_fusion.2
  53.6 17.3 %all_gather.11 = f32[3,512,128]{2,1,0:T(8,128)S(1)} all-gather(f32[3,32,128]{2,1,0:T(8,128)S(1)} %pad_maximum_fusion.33), channel_id=1, replica_groups=mesh['gx'=16,'gy'=16] {'gy'}, dimensions={1}, use_global_device_ids=true | all-gather | bytes 835584 | tf_op jit(solution)/shard_map/all_gather | solution.py:204
  71.0 1.3 fusion.245
  72.3 1.4 copy.17
  73.7 2.7 %collective-permute-start.6 = (f32[32,34,1]{1,0,2:T(8,128)S(1)}, f32[32,34,1]{1,0,2:T(8,128)S(1)}, u32[]{:S(2)}, u32[]{:S(2)}) collective-permute-start(f32[32,34,1]{1,0,2:T(8,128)S(1)} %copy.17), channel_id=1, source_target_pairs={{0,1},{1,2},{2,3},{3,4},{4,5},{5,6},{6,7},{7,8},{8,9},{9,10},{10,1... | collective-permute-start | bytes 13064 | tf_op jit(solution)/shard_map/ppermute | solution.py:20
  76.4 1.4 copy.18
  77.8 4.7 %collective-permute-start.7 = (f32[32,34,1]{1,0,2:T(8,128)S(1)}, f32[32,34,1]{1,0,2:T(8,128)}, u32[]{:S(2)}, u32[]{:S(2)}) collective-permute-start(f32[32,34,1]{1,0,2:T(8,128)S(1)} %copy.18), channel_id=1, source_target_pairs={{1,0},{2,1},{3,2},{4,3},{5,4},{6,5},{7,6},{8,7},{9,8},{10,9},{11,1... | collective-permute-start | bytes 13064 | tf_op jit(solution)/shard_map/ppermute | solution.py:21
  83.1 2.5 %fusion.242 = (f32[3,32,34,1]{3,2,1,0:T(8,128)}, f32[3,32,34,1]{3,2,1,0:T(8,128)}) fusion(f32[3,32,34,128]{3,2,1,0:T(8,128)S(1)} %pad_maximum_fusion.1), kind=kLoop, calls=%fused_computation.709 | loop fusion | bytes 52224 | tf_op jit(solution)/shard_map/slice | solution.py:18
  85.6 2.9 %copy.13 = f32[3,32,34,1]{2,1,3,0:T(8,128)} copy(f32[3,32,34,1]{3,2,1,0:T(8,128)} %get-tuple-element.160) | data formatting | bytes 26112 | tf_op jit(solution)/shard_map/slice | solution.py:18
  88.6 2.0 %collective-permute-start.2 = (f32[3,32,34,1]{2,1,3,0:T(8,128)}, f32[3,32,34,1]{2,1,3,0:T(8,128)}, u32[]{:S(2)}, u32[]{:S(2)}) collective-permute-start(f32[3,32,34,1]{2,1,3,0:T(8,128)} %copy.13), channel_id=1, source_target_pairs={{0,1},{1,2},{2,3},{3,4},{4,5},{5,6},{6,7},{7,8},{8,9},{9,10},{10,1... | collective-permute-start | bytes 39176 | tf_op jit(solution)/shard_map/ppermute | solution.py:20
  90.6 2.9 %copy.14 = f32[3,32,34,1]{2,1,3,0:T(8,128)} copy(f32[3,32,34,1]{3,2,1,0:T(8,128)} %get-tuple-element.161) | data formatting | bytes 26112 | tf_op jit(solution)/shard_map/slice | solution.py:19
  93.5 5.6 %collective-permute-start.3 = (f32[3,32,34,1]{2,1,3,0:T(8,128)}, f32[3,32,34,1]{2,1,3,0:T(8,128)}, u32[]{:S(2)}, u32[]{:S(2)}) collective-permute-start(f32[3,32,34,1]{2,1,3,0:T(8,128)} %copy.14), channel_id=1, source_target_pairs={{1,0},{2,1},{3,2},{4,3},{5,4},{6,5},{7,6},{8,7},{9,8},{10,9},{11,1... | collective-permute-start | bytes 39176 | tf_op jit(solution)/shard_map/ppermute | solution.py:21
  99.2 0.4 convolution_bitcast_fusion
  99.6 0.6 slice.1559
  100.2 0.3 copy.19
  100.6 1.1 copy.20
  101.7 2.9 %copy.15 = f32[3,32,34,1]{3,2,1,0:T(8,128)} copy(f32[3,32,34,1]{2,1,3,0:T(8,128)} %collective-permute-done.2) | data formatting | bytes 26112 | tf_op jit(solution)/shard_map/ppermute | solution.py:20
  104.5 2.8 %copy.16 = f32[3,32,34,1]{3,2,1,0:T(8,128)} copy(f32[3,32,34,1]{2,1,3,0:T(8,128)} %collective-permute-done.3) | data formatting | bytes 26112 | tf_op jit(solution)/shard_map/ppermute | solution.py:21
  107.4 5.0 %pad_maximum_fusion = f32[3,32,34,130]{3,2,1,0:T(8,128)S(1)} fusion(f32[3,32,34,1]{3,2,1,0:T(8,128)} %copy.16, f32[3,32,1,128]{3,2,1,0:T(1,128)} %copy-done.10, f32[1,32,32,128]{3,2,1,0:T(8,128)S(1)} %add_bitcast_fusion, f32[1,32,32,128]{3,2,1,0:T(8,128)S(1)} %bitcast.33, f32[1,32,32,128]{3,2,1,0:T(8,128)S(1)} %bitcast.36, ...), kind=kLoop, calls=%fused_computation | loop fusion | flops 2545920 | bytes 3394560 | tf_op jit(solution)/shard_map/concatenate | solution.py:22
  112.4 0.8 fusion.5
  113.2 1.0 copy-done.1
  114.2 0.3 add_multiply_fusion
  114.6 1.1 add_add_fusion.1
  116.1 0.4 copy-done.11
  116.5 1.6 fusion.18
  119.0 19.8 %collective-permute-start.8 = (f32[32,1,128]{2,1,0:T(1,128)S(1)}, f32[32,1,128]{2,1,0:T(1,128)S(1)}, u32[]{:S(2)}, u32[]{:S(2)}) collective-permute-start(f32[32,1,128]{2,1,0:T(1,128)S(1)} %get-tuple-element.172), channel_id=1, source_target_pairs={{0,16},{16,32},{32,48},{48,64},{64,80},{80,96},{96,112},{112,128},... | collective-permute-start | bytes 49160 | tf_op jit(solution)/shard_map/ppermute | solution.py:20
  138.8 1.9 collective-permute-start.9
  140.8 4.3 %collective-permute-done.9 = f32[32,1,128]{2,1,0:T(1,128)S(1)} collective-permute-done((f32[32,1,128]{2,1,0:T(1,128)S(1)}, f32[32,1,128]{2,1,0:T(1,128)S(1)}, u32[]{:S(2)}, u32[]{:S(2)}) %collective-permute-start.9) | collective-permute-done | bytes 16416 | tf_op jit(solution)/shard_map/ppermute | solution.py:21
  145.8 1.9 collective-permute-start.10
  147.7 0.3 copy.24
  148.0 5.7 %collective-permute-start.11 = (f32[32,34,1]{1,0,2:T(8,128)S(1)}, f32[32,34,1]{1,0,2:T(8,128)S(1)}, u32[]{:S(2)}, u32[]{:S(2)}) collective-permute-start(f32[32,34,1]{1,0,2:T(8,128)S(1)} %copy.24), channel_id=1, source_target_pairs={{1,0},{2,1},{3,2},{4,3},{5,4},{6,5},{7,6},{8,7},{9,8},{10,9},{11,1... | collective-permute-start | bytes 13064 | tf_op jit(solution)/shard_map/ppermute | solution.py:21
  153.7 0.4 copy.25
  154.3 0.3 copy.26
  154.7 2.1 %fusion.11 = f32[32,34,130]{2,1,0:T(8,128)S(1)} fusion(f32[32,34,1]{2,1,0:T(8,128)S(1)} %copy.26, f32[32,1,128]{2,1,0:T(1,128)S(1)} %collective-permute-done.9, f32[32,32,128]{2,1,0:T(8,128)S(1)} %add.405, f32[32,1,128]{2,1,0:T(1,128)S(1)} %collective-permute-done.8, f32[32,34,1]{2,1,0:T(8,128)S(1)} %copy.25, f32[3,32,34,130]{3,2,1,0:T(8,128)} %copy-done.1), kind=kLoop, calls=%fused_computation.18 | loop fusion | flops 1414400 | bytes 1697280 | tf_op jit(solution)/shard_map/mul | solution.py:32
  156.8 0.3 fusion.111
  157.1 1.1 add_add_fusion
  158.6 1.7 fusion.19
  161.2 3.1 %collective-permute-start.12 = (f32[32,1,128]{2,1,0:T(1,128)S(1)}, f32[32,1,128]{2,1,0:T(1,128)S(1)}, u32[]{:S(2)}, u32[]{:S(2)}) collective-permute-start(f32[32,1,128]{2,1,0:T(1,128)S(1)} %get-tuple-element.170), channel_id=1, source_target_pairs={{0,16},{16,32},{32,48},{48,64},{64,80},{80,96},{96,112},{112,128},... | collective-permute-start | bytes 49160 | tf_op jit(solution)/shard_map/ppermute | solution.py:20
  164.3 1.9 collective-permute-start.13
  166.3 0.6 pad_maximum_fusion.34
  166.9 3.7 %collective-permute-done.13 = f32[32,1,128]{2,1,0:T(1,128)S(1)} collective-permute-done((f32[32,1,128]{2,1,0:T(1,128)S(1)}, f32[32,1,128]{2,1,0:T(1,128)S(1)}, u32[]{:S(2)}, u32[]{:S(2)}) %collective-permute-start.13) | collective-permute-done | bytes 16416 | tf_op jit(solution)/shard_map/ppermute | solution.py:21
  171.2 1.9 collective-permute-start.14
  173.1 0.3 copy.30
  173.5 6.0 %collective-permute-start.15 = (f32[32,34,1]{1,0,2:T(8,128)S(1)}, f32[32,34,1]{1,0,2:T(8,128)S(1)}, u32[]{:S(2)}, u32[]{:S(2)}) collective-permute-start(f32[32,34,1]{1,0,2:T(8,128)S(1)} %copy.30), channel_id=1, source_target_pairs={{1,0},{2,1},{3,2},{4,3},{5,4},{6,5},{7,6},{8,7},{9,8},{10,9},{11,1... | collective-permute-start | bytes 13064 | tf_op jit(solution)/shard_map/ppermute | solution.py:21
  179.5 3.0 %slice_bitcast_fusion.1 = (f32[32,34,130]{2,1,0:T(8,128)S(1)}, f32[32,34,130]{2,1,0:T(8,128)}) fusion(f32[3,32,34,130]{3,2,1,0:T(8,128)} %copy-done.1), kind=kLoop, calls=%fused_computation.3 | loop fusion | bytes 2263040 | tf_op jit(solution)/shard_map/squeeze | solution.py:216
  182.5 0.3 copy.31
  182.8 1.2 copy.32
  184.0 2.4 %fusion.17 = f32[32,34,130]{2,1,0:T(8,128)S(1)} fusion(f32[32,34,1]{2,1,0:T(8,128)} %copy.32, f32[32,1,128]{2,1,0:T(1,128)S(1)} %collective-permute-done.13, f32[32,32,128]{2,1,0:T(8,128)S(1)} %add.423, f32[32,1,128]{2,1,0:T(1,128)S(1)} %collective-permute-done.12, f32[32,34,1]{2,1,0:T(8,128)S(1)} %copy.31, f32[3,32,34,130]{3,2,1,0:T(8,128)} %copy-done.1), kind=kLoop, calls=%fused_computation.25 | loop fusion | flops 1414400 | bytes 1697280 | tf_op jit(solution)/shard_map/mul | solution.py:32
  186.4 0.6 fusion.105
  187.1 0.4 fusion.106
  187.4 0.7 copy-done.5
  188.2 4.2 %fusion.30 = (f32[32,32,128]{2,1,0:T(8,128)}, f32[32,32,128]{2,1,0:T(8,128)}) fusion(f32[2,32,128]{2,1,0:T(8,128)S(1)} %copy-done.9, f32[32,34,130]{2,1,0:T(8,128)S(1)} %copy-done.3, f32[31,32,128]{2,1,0:T(8,128)S(1)} %get-tuple-element.26, f32[32,32,128]{2,1,0:T(8,128)S(1)} %add.423, f32[32,1,128]{2,1,0:T(1,128)S(1)} %collective-permute-done.12, ...), kind=kLoop, calls=%fused_computation.49 | loop fusion | flops 12451840 | bytes 11051520 | tf_op jit(solution)/shard_map/sub | solution.py:139
  (175 shorter events, 4.7 us)
Async XLA Ops:
  0.6 1.5 copy-start.4
  0.6 1.5 copy-start.6
  0.7 9.4 %copy-start = (f32[32,32,128]{2,1,0:T(8,128)S(1)}, f32[32,32,128]{2,1,0:T(8,128)}, u32[]{:S(2)}) copy-start(f32[32,32,128]{2,1,0:T(8,128)} %param.9) | copy-start | bytes 1572868
  2.1 15.5 %copy-start.15 = (s32[32,128]{1,0:T(8,128)S(1)}, s32[32,128]{1,0:T(8,128)}, u32[]{:S(2)}) copy-start(s32[32,128]{1,0:T(8,128)} %param.16) | copy-start | bytes 49156
  2.1 15.5 %copy-start.7 = (f32[5,17]{1,0:T(8,128)S(1)}, f32[5,17]{1,0:T(8,128)}, u32[]{:S(2)}) copy-start(f32[5,17]{1,0:T(8,128)} %param.17) | copy-start | bytes 1024
  2.1 16.5 %copy-start.35 = (u32[256]{0:T(256)S(1)}, u32[256]{0:T(256)}, u32[]{:S(2)}) copy-start(u32[256]{0:T(256)} %constant.106) | copy-start | bytes 3076
  2.1 17.7 %copy-start.33 = (s32[32,1]{0,1:T(1,128)S(1)}, s32[32,1]{0,1:T(1,128)}, u32[]{:S(2)}) copy-start(s32[32,1]{0,1:T(1,128)} %param.13) | copy-start | bytes 388
  2.1 30.2 %slice-start = ((f32[32,32,128]{2,1,0:T(8,128)}), f32[2,32,128]{2,1,0:T(8,128)S(1)}, s32[]{:S(2)}) async-start(f32[32,32,128]{2,1,0:T(8,128)} %param.9), calls=%async_computation | async-start | bytes 65536 | tf_op jit(solution)/shard_map/slice | solution.py:191
  2.8 79.6 %collective-permute-start = (f32[3,32,1,128]{3,2,1,0:T(1,128)}, f32[3,32,1,128]{3,2,1,0:T(1,128)S(1)}, u32[]{:S(2)}, u32[]{:S(2)}) collective-permute-start(f32[3,32,1,128]{3,2,1,0:T(1,128)} %get-tuple-element.162), channel_id=1, source_target_pairs={{0,16},{16,32},{32,48},{48,64},{64,80},{80,96},{96,112},{112,128},... | collective-permute-start | bytes 147464 | tf_op jit(solution)/shard_map/ppermute | solution.py:20
  8.2 74.3 %collective-permute-start.1 = (f32[3,32,1,128]{3,2,1,0:T(1,128)S(1)}, f32[3,32,1,128]{3,2,1,0:T(1,128)S(1)}, u32[]{:S(2)}, u32[]{:S(2)}) collective-permute-start(f32[3,32,1,128]{3,2,1,0:T(1,128)S(1)} %get-tuple-element.163), channel_id=1, source_target_pairs={{16,0},{32,16},{48,32},{64,48},{80,64},{96,80},{112,96},{128,112},... | collective-permute-start | bytes 147464 | tf_op jit(solution)/shard_map/ppermute | solution.py:21
  10.7 60.2 %collective-permute-start.4 = (f32[32,1,128]{2,1,0:T(1,128)}, f32[32,1,128]{2,1,0:T(1,128)S(1)}, u32[]{:S(2)}, u32[]{:S(2)}) collective-permute-start(f32[32,1,128]{2,1,0:T(1,128)} %get-tuple-element.174), channel_id=1, source_target_pairs={{0,16},{16,32},{32,48},{48,64},{64,80},{80,96},{96,112},{112,128},... | collective-permute-start | bytes 49160 | tf_op jit(solution)/shard_map/ppermute | solution.py:20
  15.6 55.3 %collective-permute-start.5 = (f32[32,1,128]{2,1,0:T(1,128)}, f32[32,1,128]{2,1,0:T(1,128)S(1)}, u32[]{:S(2)}, u32[]{:S(2)}) collective-permute-start(f32[32,1,128]{2,1,0:T(1,128)} %get-tuple-element.175), channel_id=1, source_target_pairs={{16,0},{32,16},{48,32},{64,48},{80,64},{96,80},{112,96},{128,112},... | collective-permute-start | bytes 49160 | tf_op jit(solution)/shard_map/ppermute | solution.py:21
  17.5 34.7 %copy-start.12 = (f32[7,32,128]{2,1,0:T(8,128)S(1)}, f32[7,32,128]{2,1,0:T(8,128)}, u32[]{:S(2)}) copy-start(f32[7,32,128]{2,1,0:T(8,128)} %param.14) | copy-start | bytes 344068
  32.1 19.7 %copy-start.16 = (f32[5]{0:T(128)S(1)}, f32[5]{0:T(128)}, u32[]{:S(2)}) copy-start(f32[5]{0:T(128)} %get-tuple-element.4) | copy-start | bytes 64
  32.1 19.7 %copy-start.17 = (f32[5]{0:T(128)S(1)}, f32[5]{0:T(128)}, u32[]{:S(2)}) copy-start(f32[5]{0:T(128)} %get-tuple-element.5) | copy-start | bytes 64
  32.2 19.7 %copy-start.18 = (f32[5]{0:T(128)S(1)}, f32[5]{0:T(128)}, u32[]{:S(2)}) copy-start(f32[5]{0:T(128)} %get-tuple-element.6) | copy-start | bytes 64
  32.2 19.7 %copy-start.19 = (f32[5]{0:T(128)S(1)}, f32[5]{0:T(128)}, u32[]{:S(2)}) copy-start(f32[5]{0:T(128)} %get-tuple-element.7) | copy-start | bytes 64
  32.2 19.7 %copy-start.20 = (f32[5]{0:T(128)S(1)}, f32[5]{0:T(128)}, u32[]{:S(2)}) copy-start(f32[5]{0:T(128)} %get-tuple-element.8) | copy-start | bytes 64
  32.2 19.7 %copy-start.21 = (f32[5]{0:T(128)S(1)}, f32[5]{0:T(128)}, u32[]{:S(2)}) copy-start(f32[5]{0:T(128)} %get-tuple-element.9) | copy-start | bytes 64
  32.2 19.7 %copy-start.22 = (f32[5]{0:T(128)S(1)}, f32[5]{0:T(128)}, u32[]{:S(2)}) copy-start(f32[5]{0:T(128)} %get-tuple-element.10) | copy-start | bytes 64
  32.2 19.7 %copy-start.23 = (f32[5]{0:T(128)S(1)}, f32[5]{0:T(128)}, u32[]{:S(2)}) copy-start(f32[5]{0:T(128)} %get-tuple-element.11) | copy-start | bytes 64
  32.2 19.7 %copy-start.24 = (f32[5]{0:T(128)S(1)}, f32[5]{0:T(128)}, u32[]{:S(2)}) copy-start(f32[5]{0:T(128)} %get-tuple-element.12) | copy-start | bytes 64
  32.2 19.7 %copy-start.25 = (f32[5]{0:T(128)S(1)}, f32[5]{0:T(128)}, u32[]{:S(2)}) copy-start(f32[5]{0:T(128)} %get-tuple-element.13) | copy-start | bytes 64
  32.2 19.7 %copy-start.26 = (f32[5]{0:T(128)S(1)}, f32[5]{0:T(128)}, u32[]{:S(2)}) copy-start(f32[5]{0:T(128)} %get-tuple-element.14) | copy-start | bytes 64
  32.2 19.7 %copy-start.27 = (f32[5]{0:T(128)S(1)}, f32[5]{0:T(128)}, u32[]{:S(2)}) copy-start(f32[5]{0:T(128)} %get-tuple-element.15) | copy-start | bytes 64
  32.2 19.7 %copy-start.28 = (f32[5]{0:T(128)S(1)}, f32[5]{0:T(128)}, u32[]{:S(2)}) copy-start(f32[5]{0:T(128)} %get-tuple-element.16) | copy-start | bytes 64
  32.2 19.7 %copy-start.29 = (f32[5]{0:T(128)S(1)}, f32[5]{0:T(128)}, u32[]{:S(2)}) copy-start(f32[5]{0:T(128)} %get-tuple-element.17) | copy-start | bytes 64
  32.3 19.7 %copy-start.30 = (f32[5]{0:T(128)S(1)}, f32[5]{0:T(128)}, u32[]{:S(2)}) copy-start(f32[5]{0:T(128)} %get-tuple-element.18) | copy-start | bytes 64
  32.3 19.7 %copy-start.31 = (f32[5]{0:T(128)S(1)}, f32[5]{0:T(128)}, u32[]{:S(2)}) copy-start(f32[5]{0:T(128)} %get-tuple-element.19) | copy-start | bytes 64
  32.3 19.7 %copy-start.32 = (f32[5]{0:T(128)S(1)}, f32[5]{0:T(128)}, u32[]{:S(2)}) copy-start(f32[5]{0:T(128)} %get-tuple-element.20) | copy-start | bytes 64
  73.7 26.5 %collective-permute-start.6 = (f32[32,34,1]{1,0,2:T(8,128)S(1)}, f32[32,34,1]{1,0,2:T(8,128)S(1)}, u32[]{:S(2)}, u32[]{:S(2)}) collective-permute-start(f32[32,34,1]{1,0,2:T(8,128)S(1)} %copy.17), channel_id=1, source_target_pairs={{0,1},{1,2},{2,3},{3,4},{4,5},{5,6},{6,7},{7,8},{8,9},{9,10},{10,1... | collective-permute-start | bytes 13064 | tf_op jit(solution)/shard_map/ppermute | solution.py:20
  77.8 22.8 %collective-permute-start.7 = (f32[32,34,1]{1,0,2:T(8,128)S(1)}, f32[32,34,1]{1,0,2:T(8,128)}, u32[]{:S(2)}, u32[]{:S(2)}) collective-permute-start(f32[32,34,1]{1,0,2:T(8,128)S(1)} %copy.18), channel_id=1, source_target_pairs={{1,0},{2,1},{3,2},{4,3},{5,4},{6,5},{7,6},{8,7},{9,8},{10,9},{11,1... | collective-permute-start | bytes 13064 | tf_op jit(solution)/shard_map/ppermute | solution.py:21
  82.5 0.6 copy-start.10
  88.6 10.6 %copy-start.34 = (s32[32,1]{0,1:T(1,128)S(1)}, s32[32,1]{0,1:T(1,128)}, u32[]{:S(2)}) copy-start(s32[32,1]{0,1:T(1,128)} %param.13) | copy-start | bytes 388
  88.6 13.1 %collective-permute-start.2 = (f32[3,32,34,1]{2,1,3,0:T(8,128)}, f32[3,32,34,1]{2,1,3,0:T(8,128)}, u32[]{:S(2)}, u32[]{:S(2)}) collective-permute-start(f32[3,32,34,1]{2,1,3,0:T(8,128)} %copy.13), channel_id=1, source_target_pairs={{0,1},{1,2},{2,3},{3,4},{4,5},{5,6},{6,7},{7,8},{8,9},{9,10},{10,1... | collective-permute-start | bytes 39176 | tf_op jit(solution)/shard_map/ppermute | solution.py:20
  93.5 11.0 %collective-permute-start.3 = (f32[3,32,34,1]{2,1,3,0:T(8,128)}, f32[3,32,34,1]{2,1,3,0:T(8,128)}, u32[]{:S(2)}, u32[]{:S(2)}) collective-permute-start(f32[3,32,34,1]{2,1,3,0:T(8,128)} %copy.14), channel_id=1, source_target_pairs={{1,0},{2,1},{3,2},{4,3},{5,4},{6,5},{7,6},{8,7},{9,8},{10,9},{11,1... | collective-permute-start | bytes 39176 | tf_op jit(solution)/shard_map/ppermute | solution.py:21
  99.6 59.0 %copy-start.8 = (f32[2,32,128]{2,1,0:T(8,128)}, f32[2,32,128]{2,1,0:T(8,128)S(1)}, u32[]{:S(2)}) copy-start(f32[2,32,128]{2,1,0:T(8,128)S(1)} %slice.1558) | copy-start | bytes 98308
  112.4 1.9 copy-start.1
  115.7 0.7 copy-start.11
  119.0 21.8 %collective-permute-start.8 = (f32[32,1,128]{2,1,0:T(1,128)S(1)}, f32[32,1,128]{2,1,0:T(1,128)S(1)}, u32[]{:S(2)}, u32[]{:S(2)}) collective-permute-start(f32[32,1,128]{2,1,0:T(1,128)S(1)} %get-tuple-element.172), channel_id=1, source_target_pairs={{0,16},{16,32},{32,48},{48,64},{64,80},{80,96},{96,112},{112,128},... | collective-permute-start | bytes 49160 | tf_op jit(solution)/shard_map/ppermute | solution.py:20
  138.8 6.3 %collective-permute-start.9 = (f32[32,1,128]{2,1,0:T(1,128)S(1)}, f32[32,1,128]{2,1,0:T(1,128)S(1)}, u32[]{:S(2)}, u32[]{:S(2)}) collective-permute-start(f32[32,1,128]{2,1,0:T(1,128)S(1)} %get-tuple-element.173), channel_id=1, source_target_pairs={{16,0},{32,16},{48,32},{64,48},{80,64},{96,80},{112,96},{128,112},... | collective-permute-start | bytes 49160 | tf_op jit(solution)/shard_map/ppermute | solution.py:21
  145.8 7.9 %collective-permute-start.10 = (f32[32,34,1]{1,0,2:T(8,128)S(1)}, f32[32,34,1]{1,0,2:T(8,128)S(1)}, u32[]{:S(2)}, u32[]{:S(2)}) collective-permute-start(f32[32,34,1]{1,0,2:T(8,128)S(1)} %copy.23), channel_id=1, source_target_pairs={{0,1},{1,2},{2,3},{3,4},{4,5},{5,6},{6,7},{7,8},{8,9},{9,10},{10,1... | collective-permute-start | bytes 13064 | tf_op jit(solution)/shard_map/ppermute | solution.py:20
  148.0 6.3 %collective-permute-start.11 = (f32[32,34,1]{1,0,2:T(8,128)S(1)}, f32[32,34,1]{1,0,2:T(8,128)S(1)}, u32[]{:S(2)}, u32[]{:S(2)}) collective-permute-start(f32[32,34,1]{1,0,2:T(8,128)S(1)} %copy.24), channel_id=1, source_target_pairs={{1,0},{2,1},{3,2},{4,3},{5,4},{6,5},{7,6},{8,7},{9,8},{10,9},{11,1... | collective-permute-start | bytes 13064 | tf_op jit(solution)/shard_map/ppermute | solution.py:21
  161.0 5.2 %copy-start.13 = (f32[1,32,128]{2,1,0:T(8,128)S(1)}, f32[1,32,128]{2,1,0:T(8,128)}, u32[]{:S(2)}) copy-start(f32[1,32,128]{2,1,0:T(8,128)} %get-tuple-element.21) | copy-start | bytes 49156
  161.0 5.2 %copy-start.14 = (f32[1,32,128]{2,1,0:T(8,128)S(1)}, f32[1,32,128]{2,1,0:T(8,128)}, u32[]{:S(2)}) copy-start(f32[1,32,128]{2,1,0:T(8,128)} %get-tuple-element.23) | copy-start | bytes 49156
  161.2 26.2 %copy-start.2 = (f32[32,32,128]{2,1,0:T(8,128)}, f32[32,32,128]{2,1,0:T(8,128)S(1)}, u32[]{:S(2)}) copy-start(f32[32,32,128]{2,1,0:T(8,128)S(1)} %add.423) | copy-start | bytes 1572868
  161.2 5.6 %collective-permute-start.12 = (f32[32,1,128]{2,1,0:T(1,128)S(1)}, f32[32,1,128]{2,1,0:T(1,128)S(1)}, u32[]{:S(2)}, u32[]{:S(2)}) collective-permute-start(f32[32,1,128]{2,1,0:T(1,128)S(1)} %get-tuple-element.170), channel_id=1, source_target_pairs={{0,16},{16,32},{32,48},{48,64},{64,80},{80,96},{96,112},{112,128},... | collective-permute-start | bytes 49160 | tf_op jit(solution)/shard_map/ppermute | solution.py:20
  164.3 6.3 %collective-permute-start.13 = (f32[32,1,128]{2,1,0:T(1,128)S(1)}, f32[32,1,128]{2,1,0:T(1,128)S(1)}, u32[]{:S(2)}, u32[]{:S(2)}) collective-permute-start(f32[32,1,128]{2,1,0:T(1,128)S(1)} %get-tuple-element.171), channel_id=1, source_target_pairs={{16,0},{32,16},{48,32},{64,48},{80,64},{96,80},{112,96},{128,112},... | collective-permute-start | bytes 49160 | tf_op jit(solution)/shard_map/ppermute | solution.py:21
  171.2 11.3 %collective-permute-start.14 = (f32[32,34,1]{1,0,2:T(8,128)S(1)}, f32[32,34,1]{1,0,2:T(8,128)S(1)}, u32[]{:S(2)}, u32[]{:S(2)}) collective-permute-start(f32[32,34,1]{1,0,2:T(8,128)S(1)} %copy.29), channel_id=1, source_target_pairs={{0,1},{1,2},{2,3},{3,4},{4,5},{5,6},{6,7},{7,8},{8,9},{9,10},{10,1... | collective-permute-start | bytes 13064 | tf_op jit(solution)/shard_map/ppermute | solution.py:20
  173.5 9.4 %collective-permute-start.15 = (f32[32,34,1]{1,0,2:T(8,128)S(1)}, f32[32,34,1]{1,0,2:T(8,128)S(1)}, u32[]{:S(2)}, u32[]{:S(2)}) collective-permute-start(f32[32,34,1]{1,0,2:T(8,128)S(1)} %copy.30), channel_id=1, source_target_pairs={{1,0},{2,1},{3,2},{4,3},{5,4},{6,5},{7,6},{8,7},{9,8},{10,9},{11,1... | collective-permute-start | bytes 13064 | tf_op jit(solution)/shard_map/ppermute | solution.py:21
  184.0 2.4 %copy-start.3 = (f32[32,34,130]{2,1,0:T(8,128)S(1)}, f32[32,34,130]{2,1,0:T(8,128)}, u32[]{:S(2)}) copy-start(f32[32,34,130]{2,1,0:T(8,128)} %get-tuple-element.159) | copy-start | bytes 1697284
  187.1 1.1 copy-start.5
  187.1 1.1 copy-start.9
where the time goes:
time: 194 us; the launch traced here: 192 us
  starting transfers between devices  71.3 us (37%)
  blocking collectives  47.9 us (25%)
  local copies, waits for them, and re-layouts  32.2 us (17%)
  other arithmetic  28.4 us (15%)
  waiting for transfers between devices  8.33 us (4%)
  between operations  2.62 us (1%)
    ppermute x8, starting transfers between devices, padded(): before = lax.ppermute(last, axis, up)  41.6 us
    ppermute x8, starting transfers between devices, padded(): after = lax.ppermute(first, axis, down)  29.7 us
    all_gather x1, blocking collectives, shards(): lax.all_gather(top_fields, 'gy', axis=1, tiled=True)  18.4 us
    all_gather x1, blocking collectives, shards(): all_fluxes = lax.all_gather(land_fluxes, 'gy', axis=1, tiled=True)  17.3 us
    unnamed x1, blocking collectives  12.2 us
    slice x11, local copies, waits for them, and re-layouts, padded(): last = lax.slice_in_dim(shard, length - width, length, axis=dim)  9.89 us
    ppermute x8, waiting for transfers between devices, padded(): after = lax.ppermute(first, axis, down)  8.31 us
    concatenate x5, other arithmetic, padded(): shard = jnp.concatenate([before, shard, after], axis=dim)  5.54 us
  transfers between devices with their start and end apart: 16, of which 3 were waited for; matrix products, arithmetic and copies ran while one was open for 15% of the time, Pallas kernels for 0%

commit v1 on v0

v1 whole, which is shorter than its diff:
```python
import functools
import math

import jax
import jax.numpy as jnp
from jax import lax
from jax.experimental import pallas as pl
from jax.experimental.pallas import tpu as pltpu
from jax.sharding import PartitionSpec as P

LANES = 128
HALF = 64
PAD = 8
SLOTS = 4
F32 = jnp.float32
BF16 = jnp.bfloat16
MESH = pl.DeviceIdType.MESH


def sigmoid(x):
    return 0.5 * jnp.tanh(0.5 * x) + 0.5


def root_conduct(s, ksat):
    x = ksat * (0.05 + s * s)
    return x * lax.rsqrt(x)


def iota(shape, dim):
    return lax.broadcasted_iota(jnp.int32, shape, dim)


def pieces(x):
    high = x.astype(BF16)
    rest = x - high.astype(F32)
    mid = rest.astype(BF16)
    return high, mid, (rest - mid.astype(F32)).astype(BF16)


def pick_rows(one_hot, x):
    n = x.shape[1]
    out = jnp.dot(one_hot.astype(BF16), jnp.concatenate(pieces(x), axis=1), preferred_element_type=F32)
    return (out[:, 2 * n:] + out[:, n:2 * n]) + out[:, :n]


def kernel(
    Z, X, GX, GY,
    p_hbm, k_hbm, a_hbm, v_hbm, remap_hbm, forc_hbm, state_hbm, veg_hbm, table_hbm,
    p_out, a_out, v_out, land_out,
    rp, wp, ap, mp, dg, rs, pc, ks, s0, sc, gg, yy, kvs, age, var, av, vv,
    remap, forc, state, veg, table, landn,
    osend, orecv, fsend, frecv,
    lsend, lrecv, usend, urecv, dsend, drecv,
    load_sem, out_sem, o_ssem, o_rsem, f_ssem, f_rsem, h_ssem, h_rsem,
):
    gx, gy = lax.axis_index("gx"), lax.axis_index("gy")
    up, down = lax.rem(gx + GX - 1, GX), lax.rem(gx + 1, GX)
    left, right = lax.rem(gy + GY - 1, GY), lax.rem(gy + 1, GY)
    stride = X + 2 * PAD
    side = math.isqrt(GY)

    def layer(k, shift=0):
        return pl.ds(pl.multiple_of(k * stride, 8) + (PAD + shift), X)

    def block(k):
        return pl.ds(pl.multiple_of(k * X, 8), X)

    def far(o):
        dy, dx = o // side, o % side
        return min(dy, side - dy) + min(dx, side - dx)

    offsets = sorted(range(1, GY), key=lambda o: -far(o))
    my_y, my_x = gy // side, lax.rem(gy, side)
    peers = {
        o: lax.rem(my_y + o // side, side) * side + lax.rem(my_x + o % side, side) for o in offsets
    }

    def load(src, dst, n):
        c = pltpu.make_async_copy(src, dst, load_sem.at[n])
        c.start()
        return c

    barrier = pltpu.get_barrier_semaphore()
    for o in offsets:
        pl.semaphore_signal(barrier, inc=1, device_id={"gy": peers[o]}, device_id_type=MESH)
    for d in (up, down):
        pl.semaphore_signal(barrier, inc=1, device_id={"gx": d}, device_id_type=MESH)
    c_remap = load(remap_hbm, remap, 0)
    c_forc = load(forc_hbm, forc, 3)
    c_state = load(state_hbm, state, 4)
    c_veg = load(veg_hbm, veg, 5)
    c_table = load(table_hbm, table, 6)
    c_p = load(p_hbm, pc, 1)
    c_k = load(k_hbm, ks, 2)
    c_a = load(a_hbm, age, 7)
    c_v = load(v_hbm, var, 8)

    def send(src, dst, ssem, rsem, where):
        c = pltpu.make_async_remote_copy(
            src_ref=src, dst_ref=dst, send_sem=ssem, recv_sem=rsem,
            device_id=where, device_id_type=MESH,
        )
        c.start()
        return c

    lane = iota((X, LANES), 1)
    pair = lane >> 1
    first_lane, last_lane = lane == 0, lane == LANES - 1
    edge = first_lane | last_lane
    even = (lane & 1) == 0
    zero = jnp.zeros((X, LANES), F32)
    pad = jnp.zeros((PAD, LANES), F32)

    c_remap.wait()
    bits = X.bit_length() - 1
    code_row = remap[...]
    eye = iota((X, X), 0) == iota((X, X), 1)
    code_col = jnp.sum(jnp.where(eye, jnp.broadcast_to(code_row, (X, X)), 0), axis=1, keepdims=True)
    dest_row, dest_col = code_row >> bits, code_col >> bits
    slot_col = code_col & (X - 1)
    same = jnp.broadcast_to(dest_col, (X, X)) == jnp.broadcast_to(dest_row, (X, X))
    rank_row = jnp.sum(jnp.where(same & (iota((X, X), 0) < iota((X, X), 1)), 1, 0), axis=0, keepdims=True)
    rank_col = jnp.sum(jnp.where(same & (iota((X, X), 1) < iota((X, X), 0)), 1, 0), axis=1, keepdims=True)
    rows = 8 * GY
    row_id = iota((rows, X), 0)
    row_key = (row_id >> 3) * SLOTS + (row_id & (SLOTS - 1))
    tile_of_row = (row_key == jnp.broadcast_to(dest_row * SLOTS + rank_row, (rows, X))).astype(BF16)
    slot_of_tile = (jnp.broadcast_to(slot_col, (X, LANES)) == iota((X, LANES), 1)).astype(BF16)
    osend[...] = jnp.dot(tile_of_row, slot_of_tile, preferred_element_type=F32).reshape(GY, 8, LANES)

    pl.semaphore_wait(barrier, GY + 1)

    sends = []
    o_copies = [
        send(osend.at[peers[o]], orecv.at[gy], o_ssem.at[o], o_rsem.at[o], {"gy": peers[o]}) for o in offsets
    ]
    sends += o_copies
    orecv[gy] = osend[gy]

    row_of_tile = jnp.broadcast_to(dest_col * 8 + rank_col, (X, rows))
    take = jnp.concatenate(
        [(row_of_tile + n == iota((X, rows), 1)).astype(F32) for n in (0, SLOTS)], axis=0
    )

    c_veg.wait()
    c_table.wait()
    c_forc.wait()
    c_state.wait()
    cls = veg[...]
    nveg = table.shape[1]
    par = [jnp.full((X, LANES), table[i, 0], F32) for i in range(5)]
    for v in range(1, nveg):
        hit = cls == v
        par = [jnp.where(hit, table[i, v], par[i]) for i in range(5)]
    albedo, conduct, capacity, et_factor, decay = par
    skin = (state[0] + 0.5 * ((1.0 - albedo) * 2.0 * forc[0] + 0.5 * forc[1] + forc[2])) / 1.5
    soft = jnp.maximum(skin, 0.0) + jnp.log(1.0 + jnp.exp(-jnp.abs(skin)))
    demand = conduct * soft * (1.0 + forc[4]) * (1.0 - 0.5 * forc[3]) / (0.5 + forc[5])
    wetted = state[1] + forc[6]
    drip = jnp.maximum(wetted - capacity, 0.0)
    canopy = (wetted - drip) * capacity / (demand + capacity)
    through = drip + 0.5 * forc[6]
    draw0 = 0.5 * et_factor * demand / (1.0 + decay)
    draw1 = draw0 * decay
    landn[0] = skin
    landn[1] = canopy
    c_land = pltpu.make_async_copy(landn, land_out, out_sem.at[0])
    c_land.start()
    fields = jnp.concatenate([draw0, draw1, through], axis=1)

    for ref in (rp, wp, ap, mp):
        for k in range(Z):
            ref[k * stride:k * stride + PAD, :] = pad
            ref[k * stride + PAD + X:(k + 1) * stride, :] = pad

    def edge_rows(k, n, value):
        usend[n, pl.ds(k, 1), :] = value[0:1]
        dsend[n, pl.ds(k, 1), :] = value[X - 1:X]

    def wet(k, turn):
        p = pc[k]
        s = sigmoid(p)
        r = root_conduct(s, ks[k])
        w = r * p
        (sc if turn else s0)[k] = s
        rp[layer(k), :] = r
        wp[layer(k), :] = w
        return p, s, r, w

    def near(ref, k, value):
        return (
            (ref[layer(k, -1), :] + ref[layer(k, 1), :])
            + jnp.where(first_lane, 0.0, pltpu.roll(value, 1, 1))
            + jnp.where(last_lane, 0.0, pltpu.roll(value, LANES - 1, 1))
        )

    def assemble(turn, k, c):
        p1, r1, kv1, qv1, diag1, res1 = c[:6]
        p, s, r, w = wet(k, turn)
        kv = r1 * r
        qv = kv * (p1 - p + 1.0)
        dg[block(k), :] = diag1 + kv1 + kv
        rs[block(k), :] = res1 + (qv - qv1)
        kvs[k] = kv
        sum1, sum2 = near(rp, k, r), near(wp, k, w)
        hr = 0.5 * r
        diag = 2.0 * s * (1.0 - s) + hr * sum1
        res = hr * (p * sum1 - sum2)
        if turn:
            res = res + 2.0 * (s - s0[k])
            return p, r, kv, qv, diag, res
        edge_rows(k, 0, p)
        edge_rows(k, 1, ks[k])
        acc = jnp.where(pair == k, pltpu.roll(p, 2 * k + 1, 1), c[6])
        acc = jnp.where(pair == k + HALF // 2, pltpu.roll(ks[k], HALF + 2 * k + 1, 1), acc)
        return p, r, kv, qv, diag, res, acc

    def finish(c):
        _, _, kv1, qv1, diag1, res1 = c[:6]
        dg[block(Z), :] = diag1 + kv1
        rs[block(Z), :] = res1 - qv1
        kvs[Z] = zero

    c_p.wait()
    c_k.wait()
    c = lax.fori_loop(0, Z, functools.partial(assemble, 0), (zero,) * 7, unroll=2)
    lsend[0] = c[6]
    finish(c)

    def halo(phase, row0, nrows):
        cs = [
            send(lsend.at[phase], lrecv.at[phase, 0], h_ssem.at[phase, 0], h_rsem.at[phase, 0], {"gy": right}),
            send(lsend.at[phase], lrecv.at[phase, 1], h_ssem.at[phase, 1], h_rsem.at[phase, 1], {"gy": left}),
            send(usend.at[pl.ds(row0, nrows)], urecv.at[pl.ds(row0, nrows)],
                 h_ssem.at[phase, 2], h_rsem.at[phase, 2], {"gx": up}),
            send(dsend.at[pl.ds(row0, nrows)], drecv.at[pl.ds(row0, nrows)],
                 h_ssem.at[phase, 3], h_rsem.at[phase, 3], {"gx": down}),
        ]
        sends.extend(cs)
        return cs

    h0 = halo(0, 0, 2)

    c_a.wait()
    c_v.wait()

    def moments(k, acc):
        a = age[k]
        m = var[k] + a * a
        ap[layer(k), :] = a
        mp[layer(k), :] = m
        edge_rows(k, 2, a)
        edge_rows(k, 3, m)
        acc = jnp.where(pair == k, pltpu.roll(a, 2 * k + 1, 1), acc)
        return jnp.where(pair == k + HALF // 2, pltpu.roll(m, HALF + 2 * k + 1, 1), acc)

    lsend[1] = lax.fori_loop(0, Z, moments, zero, unroll=2)
    h1 = halo(1, 2, 2)

    for c in o_copies:
        c.wait_recv()
    packed = pick_rows(orecv[...].reshape(rows, LANES)[:, :X], fields)
    low = (iota((rows, LANES), 0) & 7) < SLOTS
    first_half = jnp.where(low, packed[:, :LANES], packed[:, LANES:2 * LANES])
    fsend[:, 0:8, :] = first_half.reshape(GY, 8, LANES)
    fsend[:, 8:16, :] = packed[:, 2 * LANES:].reshape(GY, 8, LANES)
    f_copies = [
        send(fsend.at[peers[o]], frecv.at[gy], f_ssem.at[o], f_rsem.at[o], {"gy": peers[o]}) for o in offsets
    ]
    sends += f_copies
    frecv[gy] = fsend[gy]

    def lane_halo(phase):
        return jnp.where(
            even, pltpu.roll(lrecv[phase, 1], LANES - 1, 1), pltpu.roll(lrecv[phase, 0], 1, 1)
        )

    for c in h0:
        c.wait_recv()
    lane_pk = lane_halo(0)
    inside = jnp.where(even, jnp.where(gy < GY - 1, 1.0, 0.0), jnp.where(gy > 0, 1.0, 0.0))
    above_in = jnp.where(gx > 0, 1.0, 0.0)
    below_in = jnp.where(gx < GX - 1, 1.0, 0.0)

    def compact_k(packed):
        return jnp.where(lane < HALF, pltpu.roll(packed, HALF, 1), 1.0)

    edge_k = (
        (compact_k(lane_pk), compact_k(lsend[0]), inside),
        (drecv[1], usend[1], above_in),
        (urecv[1], dsend[1], below_in),
    )

    def edge_p(phase, n):
        return ((lane_halo(phase), lsend[phase]), (drecv[n], usend[n]), (urecv[n], dsend[n]))

    def edge_state(phase, n):
        out = []
        for (hk, ok, inner), (hp, op) in zip(edge_k, edge_p(phase, n)):
            hr = root_conduct(sigmoid(hp), hk) * inner
            out.append((hr, hr * hp, root_conduct(sigmoid(op), ok), op))
        return out

    def add_rows(ref, above, below):
        for row, value in ((0, above), (X - 1, below)):
            at = pl.ds(X + row, Z, stride=X)
            ref[at, :] = ref[at, :] + value

    def spread(k, compact):
        return jnp.where(edge, pltpu.roll(compact, LANES - 1 - 2 * k, 1), 0.0)

    def side_terms(phase, n):
        terms = [
            (0.5 * own_r * hr, 0.5 * own_r * (own_p * hr - hw)) for hr, hw, own_r, own_p in edge_state(phase, n)
        ]
        add_rows(dg, terms[1][0], terms[2][0])
        add_rows(rs, terms[1][1], terms[2][1])
        return terms[0]

    def eliminate(k, coupling, inv, b, lanes, source=None):
        diag = dg[block(k + 1), :] + spread(k, lanes[0])
        res = rs[block(k + 1), :] + spread(k, lanes[1])
        if source is not None:
            res = res + source
        g = coupling * inv
        b = g * b - res
        inv = 1.0 / (diag - coupling * g)
        yy[k] = b * inv
        return g, inv, b

    def from_below(lanes, k, c, source=None):
        g, inv, b = eliminate(k, kvs[k + 1], *c, lanes, source)
        gg[k + 1] = g
        return inv, b

    def update(k, n, d, acc):
        p = pc[k] + d
        pc[k] = p
        edge_rows(k, n, p)
        return jnp.where(pair == k, pltpu.roll(p, 2 * k + 1, 1), acc)

    lanes = side_terms(0, 0)
    c = lax.fori_loop(0, Z - 2, lambda i, c: from_below(lanes, Z - 1 - i, c), (zero, zero), unroll=2)
    for f in f_copies:
        f.wait_recv()
    got = pick_rows(
        take,
        jnp.concatenate(
            [frecv[:, 0:8, :].reshape(rows, LANES), frecv[:, 8:16, :].reshape(rows, LANES)], axis=1
        ),
    )
    ext0 = got[:X, :LANES] * s0[0]
    ext1 = got[X:, :LANES] * s0[1]
    fall = got[:X, LANES:]
    limit = ks[0] * (1.0 + 2.0 * (1.0 - s0[0]))
    infil = limit * fall / (limit + fall)
    c = from_below(lanes, 1, c, ext1)
    from_below(lanes, 0, c, ext0 - infil)
    d = yy[0]
    acc = update(0, 4, d, zero)

    def downward(k, c):
        d = yy[k] + gg[k] * c[0]
        return d, update(k, 4, d, c[1])

    lsend[2] = lax.fori_loop(1, Z, downward, (d, acc), unroll=2)[1]
    h2 = halo(2, 4, 1)

    c = lax.fori_loop(0, Z, functools.partial(assemble, 1), (zero,) * 6, unroll=2)
    finish(c)
    rs[block(1), :] = rs[block(1), :] + (ext0 - infil)
    rs[block(2), :] = rs[block(2), :] + ext1
    for c in h2:
        c.wait_recv()
    lanes = side_terms(2, 4)
    half = Z // 2

    def both_ends(i, c):
        inv_t, b_t, inv_b, b_b = c
        g, inv_t, b_t = eliminate(i, kvs[i], inv_t, b_t, lanes)
        gg[i] = g
        return (inv_t, b_t) + from_below(lanes, Z - 1 - i, (inv_b, b_b))

    inv_t, b_t, inv_b, b_b = lax.fori_loop(0, half, both_ends, (zero,) * 4, unroll=2)
    g = kvs[half] * inv_t
    d_b = (b_b + g * b_t) * inv_b / (1.0 - kvs[half] * g * inv_b)
    d_t = yy[half - 1] + g * d_b
    acc = update(half, 5, d_b, update(half - 1, 5, d_t, zero))

    def outward(i, c):
        d_t, d_b, acc = c
        t, b = half - 1 - i, half + i
        d_t = yy[t] + gg[t + 1] * d_t
        d_b = yy[b] + gg[b] * d_b
        return d_t, d_b, update(b, 5, d_b, update(t, 5, d_t, acc))

    lsend[3] = lax.fori_loop(1, half, outward, (d_t, d_b, acc), unroll=2)[2]
    h3 = halo(3, 5, 1)
    c_pout = pltpu.make_async_copy(pc, p_out, out_sem.at[1])
    c_pout.start()

    def flow(t, u, u_n, m, m_n):
        t_out, t_in = jnp.maximum(t, 0.0), jnp.minimum(t, 0.0)
        return t_out * u + t_in * u_n, t_out * m + t_in * m_n

    def outflows(k, c):
        p1, r1, a1, m1, ga1, gm1, out_a1, out_m1 = c
        p, s, r, w = wet(k, 1)
        a, m = ap[layer(k), :], mp[layer(k), :]
        ga, gm = flow(r1 * r * (p1 - p + 1.0), a1, a, m1, m)
        dg[block(k), :] = out_a1 + (ga - ga1)
        rs[block(k), :] = out_m1 + (gm - gm1)
        hr = 0.5 * r
        f_a, f_m = flow(
            jnp.where(last_lane, 0.0, pltpu.roll(r, LANES - 1, 1) * p - pltpu.roll(w, LANES - 1, 1)),
            a, pltpu.roll(a, LANES - 1, 1), m, pltpu.roll(m, LANES - 1, 1),
        )
        f_a, f_m = hr * f_a, hr * f_m
        u_a, u_m = flow(rp[layer(k, -1), :] * p - wp[layer(k, -1), :], a, ap[layer(k, -1), :], m, mp[layer(k, -1), :])
        d_a, d_m = flow(rp[layer(k, 1), :] * p - wp[layer(k, 1), :], a, ap[layer(k, 1), :], m, mp[layer(k, 1), :])
        out_a = hr * (u_a + d_a) + (f_a - pltpu.roll(f_a, 1, 1))
        out_m = hr * (u_m + d_m) + (f_m - pltpu.roll(f_m, 1, 1))
        return p, r, a, m, ga, gm, out_a, out_m

    c = lax.fori_loop(0, Z, outflows, (zero,) * 8)
    dg[block(Z), :] = c[6] - c[4]
    rs[block(Z), :] = c[7] - c[5]
    for k, ext in ((0, ext0), (1, ext1)):
        dg[block(k + 1), :] = dg[block(k + 1), :] + ext * ap[layer(k), :]
        rs[block(k + 1), :] = rs[block(k + 1), :] + ext * mp[layer(k), :]

    for c in h1 + h3:
        c.wait_recv()
    lane_am = lane_halo(1)
    moment_edges = (
        (lane_am, lsend[1], pltpu.roll(lane_am, HALF, 1), pltpu.roll(lsend[1], HALF, 1)),
        (drecv[2], usend[2], drecv[3], usend[3]),
        (urecv[2], dsend[2], urecv[3], dsend[3]),
    )
    terms = []
    for (hr, hw, own_r, own_p), (ha, own_a, hm, own_m) in zip(edge_state(3, 5), moment_edges):
        f_a, f_m = flow(hr * own_p - hw, own_a, ha, own_m, hm)
        terms.append((0.5 * own_r * f_a, 0.5 * own_r * f_m))
    add_rows(dg, terms[1][0], terms[2][0])
    add_rows(rs, terms[1][1], terms[2][1])

    def ages(k, _):
        a, m = age[k], mp[layer(k), :]
        out_a = dg[block(k + 1), :] + spread(k, terms[0][0])
        out_m = rs[block(k + 1), :] + spread(k, terms[0][1])
        old = 0.05 + 0.4 * s0[k]
        inv = 1.0 / (0.05 + 0.4 * sc[k])
        a2 = (old * a - 0.2 * out_a) * inv + 0.2
        av[k] = a2
        vv[k] = (old * m - 0.2 * out_m) * inv + (0.4 - a2) * a2
        return 0

    outs = []
    chunk = Z // 4
    for n in range(4):
        lax.fori_loop(n * chunk, (n + 1) * chunk, ages, 0, unroll=2)
        for i, (src, dst) in enumerate(((av, a_out), (vv, v_out))):
            at = pl.ds(n * chunk, chunk)
            c = pltpu.make_async_copy(src.at[at], dst.at[at], out_sem.at[2 + 2 * n + i])
            c.start()
            outs.append(c)
    for c in sends:
        c.wait_send()
    for c in outs + [c_land, c_pout]:
        c.wait()


def shards(GX, GY, pressure, ksat, age_mean, age_var, remap, forcing, land_state, veg_class, veg_table):
    Z, X, _ = pressure.shape
    f32 = functools.partial(jax.ShapeDtypeStruct, dtype=F32)
    padded = pltpu.VMEM((Z * (X + 2 * PAD), LANES), F32)
    flat = pltpu.VMEM(((Z + 1) * X, LANES), F32)
    plain = pltpu.VMEM((Z + 1, X, LANES), F32)
    exact = pltpu.VMEM((Z, X, LANES), F32)
    dma = pltpu.SemaphoreType.DMA
    any_spec = pl.BlockSpec(memory_space=pl.ANY)
    return pl.pallas_call(
        functools.partial(kernel, Z, X, GX, GY),
        out_shape=(
            f32((Z, X, LANES)), f32((Z, X, LANES)), f32((Z, X, LANES)), f32(land_state.shape),
        ),
        in_specs=[any_spec] * 9,
        out_specs=(any_spec,) * 4,
        scratch_shapes=[padded] * 4 + [flat] * 2 + [exact] * 4 + [plain] * 3 + [exact] * 4 + [
            pltpu.VMEM((1, X), jnp.int32),
            pltpu.VMEM(forcing.shape, F32),
            pltpu.VMEM(land_state.shape, F32),
            pltpu.VMEM(veg_class.shape, jnp.int32),
            pltpu.SMEM(veg_table.shape, F32),
            pltpu.VMEM(land_state.shape, F32),
            pltpu.VMEM((GY, 8, LANES), F32),
            pltpu.VMEM((GY, 8, LANES), F32),
            pltpu.VMEM((GY, 16, LANES), F32),
            pltpu.VMEM((GY, 16, LANES), F32),
            pltpu.VMEM((4, X, LANES), F32),
            pltpu.VMEM((4, 2, X, LANES), F32),
            pltpu.VMEM((6, Z, LANES), F32),
            pltpu.VMEM((6, Z, LANES), F32),
            pltpu.VMEM((6, Z, LANES), F32),
            pltpu.VMEM((6, Z, LANES), F32),
            dma((9,)), dma((10,)), dma((GY,)), dma((GY,)), dma((GY,)), dma((GY,)), dma((4, 4)), dma((4, 4)),
        ],
        compiler_params=pltpu.CompilerParams(
            collective_id=0, has_side_effects=True, vmem_limit_bytes=62 * 1024 * 1024
        ),
    )(pressure, ksat, age_mean, age_var, remap.reshape(1, X), forcing, land_state, veg_class, veg_table)


def solution(mesh):
    field = P(None, "gx", "gy")
    return jax.shard_map(
        functools.partial(shards, mesh.shape["gx"], mesh.shape["gy"]),
        mesh=mesh,
        in_specs=(field, field, field, field, P("gx", "gy"), field, field, P("gx", "gy"), P()),
        out_specs=(field, field, field, field),
        check_vma=False,
    )
```

time: 194 us -> 38.4 us (0.20)
  the two profiles are of different devices: /device:TPU:105 before, /device:TPU:8 now
where the time goes in v1:
time: 38.4 us; the launch traced here: 38.2 us
  Pallas kernels  33 us (86%)
  local copies, waits for them, and re-layouts  4.57 us (12%)
  between operations  0.65 us (2%)
    pallas_call x1, Pallas kernels, shards(): pl.pallas_call(functools.partial(kernel, Z, X, GX, GY), out_shape=(f32((Z...  33 us
    unnamed x10, local copies, waits for them, and re-layouts  4.57 us

profile of v1, /device:TPU:8, one launch (start us, length us, event | category | flops | bytes accessed | tf_op | source)
XLA Modules:
  0.0 38.2 jit_solution(17784366297347705800)
XLA Ops:
  0.6 33.0 %shard_map.120 = (f32[32,32,128]{2,1,0:T(8,128)}, f32[32,32,128]{2,1,0:T(8,128)}, f32[32,32,128]{2,1,0:T(8,128)}, f32[2,32,128]{2,1,0:T(8,128)}) custom-call(f32[32,32,128]{2,1,0:T(8,128)} %p_hbm.1, f32[32,32,128]{2,1,0:T(8,128)} %k_hbm.1, f32[32,32,128]{2,1,0:T(8,128)} %a_hbm.1, f32[32,32,128]{2,1,0:T(8,128)} %v_hbm.1, s32[1,32]{1,0:T(1,128)} %bitcast.1, ...), custom_call_target="tpu_custom_call" | custom-call | tf_op jit(solution)/shard_map/pallas_call | solution.py:482
  33.6 0.0 copy-start.1
  33.6 1.9 %copy.17 = f32[32,32,128]{2,1,0:T(8,128)} copy(f32[32,32,128]{2,1,0:T(8,128)} %get-tuple-element.8) | data formatting | bytes 1048576
  35.6 0.0 copy-done.1
  35.6 0.0 copy-start
  35.6 0.8 %copy.18 = f32[32,32,128]{2,1,0:T(8,128)} copy(f32[32,32,128]{2,1,0:T(8,128)S(1)} %copy-done.1) | data formatting | bytes 1048576
  36.4 0.4 %copy-done = f32[32,32,128]{2,1,0:T(8,128)S(1)} copy-done((f32[32,32,128]{2,1,0:T(8,128)S(1)}, f32[32,32,128]{2,1,0:T(8,128)}, u32[]{:S(2)}) %copy-start) | copy-done | bytes 524312
  36.8 0.0 copy-start.2
  36.8 0.8 %copy.19 = f32[32,32,128]{2,1,0:T(8,128)} copy(f32[32,32,128]{2,1,0:T(8,128)S(1)} %copy-done) | data formatting | bytes 1048576
  37.6 0.0 copy-done.2
  37.6 0.6 %copy.20 = f32[2,32,128]{2,1,0:T(8,128)} copy(f32[2,32,128]{2,1,0:T(8,128)S(1)} %copy-done.2) | data formatting | bytes 65536
Async XLA Ops:
  33.6 1.9 %copy-start.1 = (f32[32,32,128]{2,1,0:T(8,128)S(1)}, f32[32,32,128]{2,1,0:T(8,128)}, u32[]{:S(2)}) copy-start(f32[32,32,128]{2,1,0:T(8,128)} %get-tuple-element.9) | copy-start | bytes 1572868
  35.6 1.2 %copy-start = (f32[32,32,128]{2,1,0:T(8,128)S(1)}, f32[32,32,128]{2,1,0:T(8,128)}, u32[]{:S(2)}) copy-start(f32[32,32,128]{2,1,0:T(8,128)} %get-tuple-element.10) | copy-start | bytes 1572868
  36.8 0.8 %copy-start.2 = (f32[2,32,128]{2,1,0:T(8,128)S(1)}, f32[2,32,128]{2,1,0:T(8,128)}, u32[]{:S(2)}) copy-start(f32[2,32,128]{2,1,0:T(8,128)} %get-tuple-element.11) | copy-start | bytes 98308

commit v2 on v1

--- a/solution.py
+++ b/solution.py
@@ -46,12 +46,12 @@
 def kernel(
     Z, X, GX, GY,
     p_hbm, k_hbm, a_hbm, v_hbm, remap_hbm, forc_hbm, state_hbm, veg_hbm, table_hbm,
-    p_out, a_out, v_out, land_out,
-    rp, wp, ap, mp, dg, rs, pc, ks, s0, sc, gg, yy, kvs, age, var, av, vv,
-    remap, forc, state, veg, table, landn,
+    pc, landn, dg, rs, s0, sc, age, mom, terms_out,
+    rp, wp, ap, mp, ks, gg, yy, kvs, var,
+    remap, forc, state, veg, table,
     osend, orecv, fsend, frecv,
     lsend, lrecv, usend, urecv, dsend, drecv,
-    load_sem, out_sem, o_ssem, o_rsem, f_ssem, f_rsem, h_ssem, h_rsem,
+    load_sem, o_ssem, o_rsem, f_ssem, f_rsem, h_ssem, h_rsem,
 ):
     gx, gy = lax.axis_index("gx"), lax.axis_index("gy")
     up, down = lax.rem(gx + GX - 1, GX), lax.rem(gx + 1, GX)
@@ -164,8 +164,6 @@
     draw1 = draw0 * decay
     landn[0] = skin
     landn[1] = canopy
-    c_land = pltpu.make_async_copy(landn, land_out, out_sem.at[0])
-    c_land.start()
     fields = jnp.concatenate([draw0, draw1, through], axis=1)
 
     for ref in (rp, wp, ap, mp):
@@ -223,7 +221,7 @@
 
     c_p.wait()
     c_k.wait()
-    c = lax.fori_loop(0, Z, functools.partial(assemble, 0), (zero,) * 7, unroll=2)
+    c = lax.fori_loop(0, Z, functools.partial(assemble, 0), (zero,) * 7, unroll=4)
     lsend[0] = c[6]
     finish(c)
 
@@ -240,22 +238,6 @@
         return cs
 
     h0 = halo(0, 0, 2)
-
-    c_a.wait()
-    c_v.wait()
-
-    def moments(k, acc):
-        a = age[k]
-        m = var[k] + a * a
-        ap[layer(k), :] = a
-        mp[layer(k), :] = m
-        edge_rows(k, 2, a)
-        edge_rows(k, 3, m)
-        acc = jnp.where(pair == k, pltpu.roll(a, 2 * k + 1, 1), acc)
-        return jnp.where(pair == k + HALF // 2, pltpu.roll(m, HALF + 2 * k + 1, 1), acc)
-
-    lsend[1] = lax.fori_loop(0, Z, moments, zero, unroll=2)
-    h1 = halo(1, 2, 2)
 
     for c in o_copies:
         c.wait_recv()
@@ -270,6 +252,23 @@
     sends += f_copies
     frecv[gy] = fsend[gy]
 
+    c_a.wait()
+    c_v.wait()
+
+    def moments(k, acc):
+        a = age[k]
+        m = var[k] + a * a
+        ap[layer(k), :] = a
+        mp[layer(k), :] = m
+        mom[k] = m
+        edge_rows(k, 2, a)
+        edge_rows(k, 3, m)
+        acc = jnp.where(pair == k, pltpu.roll(a, 2 * k + 1, 1), acc)
+        return jnp.where(pair == k + HALF // 2, pltpu.roll(m, HALF + 2 * k + 1, 1), acc)
+
+    lsend[1] = lax.fori_loop(0, Z, moments, zero, unroll=4)
+    h1 = halo(1, 2, 2)
+
     def lane_halo(phase):
         return jnp.where(
             even, pltpu.roll(lrecv[phase, 1], LANES - 1, 1), pltpu.roll(lrecv[phase, 0], 1, 1)
@@ -340,7 +339,7 @@
         return jnp.where(pair == k, pltpu.roll(p, 2 * k + 1, 1), acc)
 
     lanes = side_terms(0, 0)
-    c = lax.fori_loop(0, Z - 2, lambda i, c: from_below(lanes, Z - 1 - i, c), (zero, zero), unroll=2)
+    c = lax.fori_loop(0, Z - 2, lambda i, c: from_below(lanes, Z - 1 - i, c), (zero, zero), unroll=4)
     for f in f_copies:
         f.wait_recv()
     got = pick_rows(
@@ -363,10 +362,10 @@
         d = yy[k] + gg[k] * c[0]
         return d, update(k, 4, d, c[1])
 
-    lsend[2] = lax.fori_loop(1, Z, downward, (d, acc), unroll=2)[1]
+    lsend[2] = lax.fori_loop(1, Z, downward, (d, acc), unroll=31)[1]
     h2 = halo(2, 4, 1)
 
-    c = lax.fori_loop(0, Z, functools.partial(assemble, 1), (zero,) * 6, unroll=2)
+    c = lax.fori_loop(0, Z, functools.partial(assemble, 1), (zero,) * 6, unroll=4)
     finish(c)
     rs[block(1), :] = rs[block(1), :] + (ext0 - infil)
     rs[block(2), :] = rs[block(2), :] + ext1
@@ -381,7 +380,7 @@
         gg[i] = g
         return (inv_t, b_t) + from_below(lanes, Z - 1 - i, (inv_b, b_b))
 
-    inv_t, b_t, inv_b, b_b = lax.fori_loop(0, half, both_ends, (zero,) * 4, unroll=2)
+    inv_t, b_t, inv_b, b_b = lax.fori_loop(0, half, both_ends, (zero,) * 4, unroll=16)
     g = kvs[half] * inv_t
     d_b = (b_b + g * b_t) * inv_b / (1.0 - kvs[half] * g * inv_b)
     d_t = yy[half - 1] + g * d_b
@@ -394,10 +393,8 @@
         d_b = yy[b] + gg[b] * d_b
         return d_t, d_b, update(b, 5, d_b, update(t, 5, d_t, acc))
 
-    lsend[3] = lax.fori_loop(1, half, outward, (d_t, d_b, acc), unroll=2)[2]
+    lsend[3] = lax.fori_loop(1, half, outward, (d_t, d_b, acc), unroll=15)[2]
     h3 = halo(3, 5, 1)
-    c_pout = pltpu.make_async_copy(pc, p_out, out_sem.at[1])
-    c_pout.start()
 
     def flow(t, u, u_n, m, m_n):
         t_out, t_in = jnp.maximum(t, 0.0), jnp.minimum(t, 0.0)
@@ -422,7 +419,7 @@
         out_m = hr * (u_m + d_m) + (f_m - pltpu.roll(f_m, 1, 1))
         return p, r, a, m, ga, gm, out_a, out_m
 
-    c = lax.fori_loop(0, Z, outflows, (zero,) * 8)
+    c = lax.fori_loop(0, Z, outflows, (zero,) * 8, unroll=2)
     dg[block(Z), :] = c[6] - c[4]
     rs[block(Z), :] = c[7] - c[5]
     for k, ext in ((0, ext0), (1, ext1)):
@@ -444,10 +441,37 @@
     add_rows(dg, terms[1][0], terms[2][0])
     add_rows(rs, terms[1][1], terms[2][1])
 
+    terms_out[0] = terms[0][0]
+    terms_out[1] = terms[0][1]
+    for c in sends:
+        c.wait_send()
+
+
+def finale(
+    Z, X, pc, landn, dg, rs, s0, sc, age, mom, terms, p_out, a_out, v_out, land_out, av, vv, out_sem
+):
+    copies = []
+
+    def store(src, dst):
+        c = pltpu.make_async_copy(src, dst, out_sem.at[len(copies)])
+        c.start()
+        copies.append(c)
+
+    store(pc, p_out)
+    store(landn, land_out)
+    lane = iota((X, LANES), 1)
+    edge = (lane == 0) | (lane == LANES - 1)
+
+    def block(k):
+        return pl.ds(pl.multiple_of(k * X, 8), X)
+
+    def spread(k, compact):
+        return jnp.where(edge, pltpu.roll(compact, LANES - 1 - 2 * k, 1), 0.0)
+
     def ages(k, _):
-        a, m = age[k], mp[layer(k), :]
-        out_a = dg[block(k + 1), :] + spread(k, terms[0][0])
-        out_m = rs[block(k + 1), :] + spread(k, terms[0][1])
+        a, m = age[k], mom[k]
+        out_a = dg[block(k + 1), :] + spread(k, terms[0])
+        out_m = rs[block(k + 1), :] + spread(k, terms[1])
         old = 0.05 + 0.4 * s0[k]
         inv = 1.0 / (0.05 + 0.4 * sc[k])
         a2 = (old * a - 0.2 * out_a) * inv + 0.2
@@ -455,18 +479,13 @@
         vv[k] = (old * m - 0.2 * out_m) * inv + (0.4 - a2) * a2
         return 0
 
-    outs = []
     chunk = Z // 4
     for n in range(4):
-        lax.fori_loop(n * chunk, (n + 1) * chunk, ages, 0, unroll=2)
-        for i, (src, dst) in enumerate(((av, a_out), (vv, v_out))):
-            at = pl.ds(n * chunk, chunk)
-            c = pltpu.make_async_copy(src.at[at], dst.at[at], out_sem.at[2 + 2 * n + i])
-            c.start()
-            outs.append(c)
-    for c in sends:
-        c.wait_send()
-    for c in outs + [c_land, c_pout]:
+        lax.fori_loop(n * chunk, (n + 1) * chunk, ages, 0, unroll=8)
+        at = pl.ds(n * chunk, chunk)
+        store(av.at[at], a_out.at[at])
+        store(vv.at[at], v_out.at[at])
+    for c in copies:
         c.wait()
 
 
@@ -476,23 +495,23 @@
     padded = pltpu.VMEM((Z * (X + 2 * PAD), LANES), F32)
     flat = pltpu.VMEM(((Z + 1) * X, LANES), F32)
     plain = pltpu.VMEM((Z + 1, X, LANES), F32)
+    land = pltpu.VMEM(land_state.shape, F32)
     exact = pltpu.VMEM((Z, X, LANES), F32)
     dma = pltpu.SemaphoreType.DMA
     any_spec = pl.BlockSpec(memory_space=pl.ANY)
-    return pl.pallas_call(
+    vmem_spec = pl.BlockSpec(memory_space=pltpu.VMEM)
+    inputs = (pressure, ksat, age_mean, age_var, remap.reshape(1, X), forcing, land_state, veg_class, veg_table)
+    held = pl.pallas_call(
         functools.partial(kernel, Z, X, GX, GY),
-        out_shape=(
-            f32((Z, X, LANES)), f32((Z, X, LANES)), f32((Z, X, LANES)), f32(land_state.shape),
-        ),
+        out_shape=(exact, land, flat, flat, exact, exact, exact, exact, pltpu.VMEM((2, X, LANES), F32)),
         in_specs=[any_spec] * 9,
-        out_specs=(any_spec,) * 4,
-        scratch_shapes=[padded] * 4 + [flat] * 2 + [exact] * 4 + [plain] * 3 + [exact] * 4 + [
+        out_specs=(vmem_spec,) * 9,
+        scratch_shapes=[padded] * 4 + [exact] + [plain] * 3 + [exact] + [
             pltpu.VMEM((1, X), jnp.int32),
             pltpu.VMEM(forcing.shape, F32),
             pltpu.VMEM(land_state.shape, F32),
             pltpu.VMEM(veg_class.shape, jnp.int32),
             pltpu.SMEM(veg_table.shape, F32),
-            pltpu.VMEM(land_state.shape, F32),
             pltpu.VMEM((GY, 8, LANES), F32),
             pltpu.VMEM((GY, 8, LANES), F32),
             pltpu.VMEM((GY, 16, LANES), F32),
@@ -503,12 +522,22 @@
             pltpu.VMEM((6, Z, LANES), F32),
             pltpu.VMEM((6, Z, LANES), F32),
             pltpu.VMEM((6, Z, LANES), F32),
-            dma((9,)), dma((10,)), dma((GY,)), dma((GY,)), dma((GY,)), dma((GY,)), dma((4, 4)), dma((4, 4)),
+            dma((9,)), dma((GY,)), dma((GY,)), dma((GY,)), dma((GY,)), dma((4, 4)), dma((4, 4)),
         ],
         compiler_params=pltpu.CompilerParams(
-            collective_id=0, has_side_effects=True, vmem_limit_bytes=62 * 1024 * 1024
+            collective_id=0, has_side_effects=True, vmem_limit_bytes=24 * 1024 * 1024
         ),
-    )(pressure, ksat, age_mean, age_var, remap.reshape(1, X), forcing, land_state, veg_class, veg_table)
+    )(*(pltpu.with_memory_space_constraint(x, pltpu.HBM) for x in inputs))
+    return pl.pallas_call(
+        functools.partial(finale, Z, X),
+        out_shape=(
+            f32((Z, X, LANES)), f32((Z, X, LANES)), f32((Z, X, LANES)), f32(land_state.shape),
+        ),
+        in_specs=[vmem_spec] * 9,
+        out_specs=(any_spec,) * 4,
+        scratch_shapes=[exact, exact, dma((10,))],
+        compiler_params=pltpu.CompilerParams(vmem_limit_bytes=8 * 1024 * 1024),
+    )(*held)
 
 
 def solution(mesh):

time: 38.4 us -> 28.9 us (0.75)
  the two profiles are of different devices: /device:TPU:8 before, /device:TPU:2 now
where the time goes in v2:
time: 28.9 us; the launch traced here: 28.8 us
  Pallas kernels  28.2 us (98%)
  between operations  0.64 us (2%)
    pallas_call x1, Pallas kernels, shards(): pl.pallas_call(functools.partial(kernel, Z, X, GX, GY), out_shape=(exact,...  26.9 us
    pallas_call x1, Pallas kernels, shards(): pl.pallas_call(functools.partial(finale, Z, X), out_shape=(f32((Z, X, LAN...  1.27 us

profile of v2, /device:TPU:2, one launch (start us, length us, event | category | flops | bytes accessed | tf_op | source)
XLA Modules:
  0.0 28.8 jit_solution(4256735139802616723)
XLA Ops:
  0.6 26.9 %shard_map.120 = (f32[32,32,128]{2,1,0:T(8,128)S(1)}, f32[2,32,128]{2,1,0:T(8,128)S(1)}, f32[1056,128]{1,0:T(8,128)S(1)}, f32[1056,128]{1,0:T(8,128)S(1)}, f32[3...) custom-call(f32[32,32,128]{2,1,0:T(8,128)} %p_hbm.1, ...), custom_call_target="tpu_custom_call" | custom-call | tf_op jit(solution)/shard_map/pallas_call | solution.py:504
  27.5 1.3 %shard_map.121 = (f32[32,32,128]{2,1,0:T(8,128)}, f32[32,32,128]{2,1,0:T(8,128)}, f32[32,32,128]{2,1,0:T(8,128)}, f32[2,32,128]{2,1,0:T(8,128)}) custom-call(f32[32,32,128]{2,1,0:T(8,128)S(1)} %get-tuple-element.13.pc, f32[2,32,128]{2,1,0:T(8,128)S(1)} %get-tuple-element.14.landn, f32[1056,128]{1,0:T(8,128)S(1)} %get-tuple-element.15.dg, ...), custom_call_target="tpu_custom_call" | custom-call | tf_op jit(solution)/shard_map/pallas_call | solution.py:531

commit v3 on v2

--- a/solution.py
+++ b/solution.py
@@ -47,9 +47,9 @@
     Z, X, GX, GY,
     p_hbm, k_hbm, a_hbm, v_hbm, remap_hbm, forc_hbm, state_hbm, veg_hbm, table_hbm,
     pc, landn, dg, rs, s0, sc, age, mom, terms_out,
-    rp, wp, ap, mp, ks, gg, yy, kvs, var,
+    rp, wp, ap, mp, ks, gg, yy, kvs, var, slope, inv1,
     remap, forc, state, veg, table,
-    osend, orecv, fsend, frecv,
+    osend, orecv, fsend, frecv, tiles,
     lsend, lrecv, usend, urecv, dsend, drecv,
     load_sem, o_ssem, o_rsem, f_ssem, f_rsem, h_ssem, h_rsem,
 ):
@@ -138,9 +138,8 @@
     orecv[gy] = osend[gy]
 
     row_of_tile = jnp.broadcast_to(dest_col * 8 + rank_col, (X, rows))
-    take = jnp.concatenate(
-        [(row_of_tile + n == iota((X, rows), 1)).astype(F32) for n in (0, SLOTS)], axis=0
-    )
+    take = (row_of_tile == iota((X, rows), 1)).astype(F32)
+    tiles[...] = jnp.zeros_like(tiles)
 
     c_veg.wait()
     c_table.wait()
@@ -175,8 +174,11 @@
         usend[n, pl.ds(k, 1), :] = value[0:1]
         dsend[n, pl.ds(k, 1), :] = value[X - 1:X]
 
-    def wet(k, turn):
+    def wet(k, turn, change=None):
         p = pc[k]
+        if change is not None:
+            p = p + slope[k] * change
+            pc[k] = p
         s = sigmoid(p)
         r = root_conduct(s, ks[k])
         w = r * p
@@ -192,9 +194,9 @@
             + jnp.where(last_lane, 0.0, pltpu.roll(value, LANES - 1, 1))
         )
 
-    def assemble(turn, k, c):
+    def assemble(turn, change, k, c):
         p1, r1, kv1, qv1, diag1, res1 = c[:6]
-        p, s, r, w = wet(k, turn)
+        p, s, r, w = wet(k, turn, change)
         kv = r1 * r
         qv = kv * (p1 - p + 1.0)
         dg[block(k), :] = diag1 + kv1 + kv
@@ -221,7 +223,7 @@
 
     c_p.wait()
     c_k.wait()
-    c = lax.fori_loop(0, Z, functools.partial(assemble, 0), (zero,) * 7, unroll=4)
+    c = lax.fori_loop(0, Z, functools.partial(assemble, 0, None), (zero,) * 7, unroll=4)
     lsend[0] = c[6]
     finish(c)
 
@@ -242,10 +244,8 @@
     for c in o_copies:
         c.wait_recv()
     packed = pick_rows(orecv[...].reshape(rows, LANES)[:, :X], fields)
-    low = (iota((rows, LANES), 0) & 7) < SLOTS
-    first_half = jnp.where(low, packed[:, :LANES], packed[:, LANES:2 * LANES])
-    fsend[:, 0:8, :] = first_half.reshape(GY, 8, LANES)
-    fsend[:, 8:16, :] = packed[:, 2 * LANES:].reshape(GY, 8, LANES)
+    for f in range(3):
+        fsend[:, f, :, :] = packed[:, f * LANES:(f + 1) * LANES].reshape(GY, 8, LANES)[:, :SLOTS, :]
     f_copies = [
         send(fsend.at[peers[o]], frecv.at[gy], f_ssem.at[o], f_rsem.at[o], {"gy": peers[o]}) for o in offsets
     ]
@@ -290,14 +290,17 @@
         (urecv[1], dsend[1], below_in),
     )
 
-    def edge_p(phase, n):
-        return ((lane_halo(phase), lsend[phase]), (drecv[n], usend[n]), (urecv[n], dsend[n]))
-
-    def edge_state(phase, n):
+    def own_state(phase, n):
+        return [
+            (0.5 * root_conduct(sigmoid(op), ok), op)
+            for (_, ok, _), op in zip(edge_k, (lsend[phase], usend[n], dsend[n]))
+        ]
+
+    def edge_state(phase, n, own):
         out = []
-        for (hk, ok, inner), (hp, op) in zip(edge_k, edge_p(phase, n)):
+        for (hk, _, inner), hp, mine in zip(edge_k, (lane_halo(phase), drecv[n], urecv[n]), own):
             hr = root_conduct(sigmoid(hp), hk) * inner
-            out.append((hr, hr * hp, root_conduct(sigmoid(op), ok), op))
+            out.append((hr, hr * hp) + mine)
         return out
 
     def add_rows(ref, above, below):
@@ -308,27 +311,25 @@
     def spread(k, compact):
         return jnp.where(edge, pltpu.roll(compact, LANES - 1 - 2 * k, 1), 0.0)
 
-    def side_terms(phase, n):
+    def side_terms(phase, n, own):
         terms = [
-            (0.5 * own_r * hr, 0.5 * own_r * (own_p * hr - hw)) for hr, hw, own_r, own_p in edge_state(phase, n)
+            (half_r * hr, half_r * (own_p * hr - hw)) for hr, hw, half_r, own_p in edge_state(phase, n, own)
         ]
         add_rows(dg, terms[1][0], terms[2][0])
         add_rows(rs, terms[1][1], terms[2][1])
         return terms[0]
 
-    def eliminate(k, coupling, inv, b, lanes, source=None):
+    def eliminate(k, coupling, inv, b, lanes):
         diag = dg[block(k + 1), :] + spread(k, lanes[0])
         res = rs[block(k + 1), :] + spread(k, lanes[1])
-        if source is not None:
-            res = res + source
         g = coupling * inv
         b = g * b - res
         inv = 1.0 / (diag - coupling * g)
         yy[k] = b * inv
         return g, inv, b
 
-    def from_below(lanes, k, c, source=None):
-        g, inv, b = eliminate(k, kvs[k + 1], *c, lanes, source)
+    def from_below(lanes, k, c):
+        g, inv, b = eliminate(k, kvs[k + 1], *c, lanes)
         gg[k + 1] = g
         return inv, b
 
@@ -338,40 +339,64 @@
         edge_rows(k, n, p)
         return jnp.where(pair == k, pltpu.roll(p, 2 * k + 1, 1), acc)
 
-    lanes = side_terms(0, 0)
-    c = lax.fori_loop(0, Z - 2, lambda i, c: from_below(lanes, Z - 1 - i, c), (zero, zero), unroll=4)
+    lanes = side_terms(0, 0, own_state(0, 0))
+    c = lax.fori_loop(0, Z - 1, lambda i, c: from_below(lanes, Z - 1 - i, c), (zero, zero), unroll=4)
+    inv1[...] = c[0]
+    c = from_below(lanes, 0, c)
+    inv0 = c[0]
+    d = yy[0]
+    acc = update(0, 4, d, zero)
+    slope[0] = zero
+    usend[6, 0:1, :] = zero[0:1]
+    dsend[6, 0:1, :] = zero[0:1]
+
+    def downward(k, c):
+        d, grow, acc, acc_g = c
+        g = gg[k]
+        d = yy[k] + g * d
+        grow = jnp.where(k > 1, g * grow, grow)
+        slope[k] = grow
+        edge_rows(k, 6, grow)
+        acc_g = jnp.where(pair == k, pltpu.roll(grow, 2 * k + 1, 1), acc_g)
+        return d, grow, update(k, 4, d, acc), acc_g
+
+    _, _, acc, acc_g = lax.fori_loop(1, Z, downward, (d, jnp.ones_like(zero), acc, zero), unroll=8)
     for f in f_copies:
         f.wait_recv()
-    got = pick_rows(
-        take,
-        jnp.concatenate(
-            [frecv[:, 0:8, :].reshape(rows, LANES), frecv[:, 8:16, :].reshape(rows, LANES)], axis=1
-        ),
-    )
-    ext0 = got[:X, :LANES] * s0[0]
-    ext1 = got[X:, :LANES] * s0[1]
-    fall = got[:X, LANES:]
+    for f in range(3):
+        tiles[f, :, :SLOTS, :] = frecv[:, f, :, :]
+    got = pick_rows(take, jnp.concatenate([tiles[f].reshape(rows, LANES) for f in range(3)], axis=1))
+    ext0 = got[:, :LANES] * s0[0]
+    ext1 = got[:, LANES:2 * LANES] * s0[1]
+    fall = got[:, 2 * LANES:]
     limit = ks[0] * (1.0 + 2.0 * (1.0 - s0[0]))
     infil = limit * fall / (limit + fall)
-    c = from_below(lanes, 1, c, ext1)
-    from_below(lanes, 0, c, ext0 - infil)
-    d = yy[0]
-    acc = update(0, 4, d, zero)
-
-    def downward(k, c):
-        d = yy[k] + gg[k] * c[0]
-        return d, update(k, 4, d, c[1])
-
-    lsend[2] = lax.fori_loop(1, Z, downward, (d, acc), unroll=31)[1]
+    d0 = -inv0 * (ext0 - infil + gg[1] * ext1)
+    d1 = gg[1] * d0 - inv1[...] * ext1
+
+    def ends(value):
+        return jnp.where(
+            even,
+            jnp.broadcast_to(value[:, LANES - 1:], (X, LANES)),
+            jnp.broadcast_to(value[:, :1], (X, LANES)),
+        )
+
+    lsend[2] = acc + acc_g * ends(d1) + jnp.where(pair == 0, ends(d0), 0.0)
+    first = iota((Z, LANES), 0) == 0
+    for ref, row in ((usend, 0), (dsend, X - 1)):
+        d0_row, d1_row = (jnp.broadcast_to(v[row:row + 1], (Z, LANES)) for v in (d0, d1))
+        ref[4] = ref[4] + ref[6] * d1_row + jnp.where(first, d0_row, 0.0)
     h2 = halo(2, 4, 1)
 
-    c = lax.fori_loop(0, Z, functools.partial(assemble, 1), (zero,) * 6, unroll=4)
+    pc[0] = pc[0] + d0
+    c = lax.fori_loop(0, Z, functools.partial(assemble, 1, d1), (zero,) * 6, unroll=4)
     finish(c)
     rs[block(1), :] = rs[block(1), :] + (ext0 - infil)
     rs[block(2), :] = rs[block(2), :] + ext1
+    own = own_state(2, 4)
     for c in h2:
         c.wait_recv()
-    lanes = side_terms(2, 4)
+    lanes = side_terms(2, 4, own)
     half = Z // 2
 
     def both_ends(i, c):
@@ -426,7 +451,8 @@
         dg[block(k + 1), :] = dg[block(k + 1), :] + ext * ap[layer(k), :]
         rs[block(k + 1), :] = rs[block(k + 1), :] + ext * mp[layer(k), :]
 
-    for c in h1 + h3:
+    own = own_state(3, 5)
+    for c in h1:
         c.wait_recv()
     lane_am = lane_halo(1)
     moment_edges = (
@@ -434,16 +460,20 @@
         (drecv[2], usend[2], drecv[3], usend[3]),
         (urecv[2], dsend[2], urecv[3], dsend[3]),
     )
+    for c in sends[:-len(h3)]:
+        c.wait_send()
+    for c in h3:
+        c.wait_recv()
     terms = []
-    for (hr, hw, own_r, own_p), (ha, own_a, hm, own_m) in zip(edge_state(3, 5), moment_edges):
+    for (hr, hw, half_r, own_p), (ha, own_a, hm, own_m) in zip(edge_state(3, 5, own), moment_edges):
         f_a, f_m = flow(hr * own_p - hw, own_a, ha, own_m, hm)
-        terms.append((0.5 * own_r * f_a, 0.5 * own_r * f_m))
+        terms.append((half_r * f_a, half_r * f_m))
     add_rows(dg, terms[1][0], terms[2][0])
     add_rows(rs, terms[1][1], terms[2][1])
 
     terms_out[0] = terms[0][0]
     terms_out[1] = terms[0][1]
-    for c in sends:
+    for c in h3:
         c.wait_send()
 
 
@@ -506,7 +536,7 @@
         out_shape=(exact, land, flat, flat, exact, exact, exact, exact, pltpu.VMEM((2, X, LANES), F32)),
         in_specs=[any_spec] * 9,
         out_specs=(vmem_spec,) * 9,
-        scratch_shapes=[padded] * 4 + [exact] + [plain] * 3 + [exact] + [
+        scratch_shapes=[padded] * 4 + [exact] + [plain] * 3 + [exact] * 2 + [pltpu.VMEM((X, LANES), F32)] + [
             pltpu.VMEM((1, X), jnp.int32),
             pltpu.VMEM(forcing.shape, F32),
             pltpu.VMEM(land_state.shape, F32),
@@ -514,13 +544,14 @@
             pltpu.SMEM(veg_table.shape, F32),
             pltpu.VMEM((GY, 8, LANES), F32),
             pltpu.VMEM((GY, 8, LANES), F32),
-            pltpu.VMEM((GY, 16, LANES), F32),
-            pltpu.VMEM((GY, 16, LANES), F32),
+            pltpu.VMEM((GY, 3, SLOTS, LANES), F32),
+            pltpu.VMEM((GY, 3, SLOTS, LANES), F32),
+            pltpu.VMEM((3, GY, 8, LANES), F32),
             pltpu.VMEM((4, X, LANES), F32),
             pltpu.VMEM((4, 2, X, LANES), F32),
+            pltpu.VMEM((7, Z, LANES), F32),
             pltpu.VMEM((6, Z, LANES), F32),
-            pltpu.VMEM((6, Z, LANES), F32),
-            pltpu.VMEM((6, Z, LANES), F32),
+            pltpu.VMEM((7, Z, LANES), F32),
             pltpu.VMEM((6, Z, LANES), F32),
             dma((9,)), dma((GY,)), dma((GY,)), dma((GY,)), dma((GY,)), dma((4, 4)), dma((4, 4)),
         ],

time: 28.9 us -> 28.6 us (0.990)
  Pallas kernels: 28.2 us -> 27.8 us
    pallas_call x1, Pallas kernels: 26.9 us -> 26.6 us  [shards(): pl.pallas_call(functools.partial(kernel, Z, X, GX, GY), out_shape=(exact,...]
where the time goes in v3:
time: 28.6 us; the launch traced here: 28.5 us
  Pallas kernels  27.8 us (97%)
  between operations  0.64 us (2%)
    pallas_call x1, Pallas kernels, shards(): pl.pallas_call(functools.partial(kernel, Z, X, GX, GY), out_shape=(exact,...  26.6 us
    pallas_call x1, Pallas kernels, shards(): pl.pallas_call(functools.partial(finale, Z, X), out_shape=(f32((Z, X, LAN...  1.27 us

profile of v3, /device:TPU:2, one launch (start us, length us, event | category | flops | bytes accessed | tf_op | source)
XLA Modules:
  0.0 28.5 jit_solution(3230211712493842837)
XLA Ops:
  0.6 26.6 %shard_map.120 = (f32[32,32,128]{2,1,0:T(8,128)S(1)}, f32[2,32,128]{2,1,0:T(8,128)S(1)}, f32[1056,128]{1,0:T(8,128)S(1)}, f32[1056,128]{1,0:T(8,128)S(1)}, f32[3...) custom-call(f32[32,32,128]{2,1,0:T(8,128)} %p_hbm.1, ...), custom_call_target="tpu_custom_call" | custom-call | tf_op jit(solution)/shard_map/pallas_call | solution.py:534
  27.2 1.3 %shard_map.121 = (f32[32,32,128]{2,1,0:T(8,128)}, f32[32,32,128]{2,1,0:T(8,128)}, f32[32,32,128]{2,1,0:T(8,128)}, f32[2,32,128]{2,1,0:T(8,128)}) custom-call(f32[32,32,128]{2,1,0:T(8,128)S(1)} %get-tuple-element.13.pc, f32[2,32,128]{2,1,0:T(8,128)S(1)} %get-tuple-element.14.landn, f32[1056,128]{1,0:T(8,128)S(1)} %get-tuple-element.15.dg, ...), custom_call_target="tpu_custom_call" | custom-call | tf_op jit(solution)/shard_map/pallas_call | solution.py:562

commit v4 on v3

--- a/solution.py
+++ b/solution.py
@@ -12,6 +12,7 @@
 HALF = 64
 PAD = 8
 SLOTS = 4
+FAR = 1
 F32 = jnp.float32
 BF16 = jnp.bfloat16
 MESH = pl.DeviceIdType.MESH
@@ -49,9 +50,9 @@
     pc, landn, dg, rs, s0, sc, age, mom, terms_out,
     rp, wp, ap, mp, ks, gg, yy, kvs, var, slope, inv1,
     remap, forc, state, veg, table,
-    osend, orecv, fsend, frecv, tiles,
+    osend, orecv, fsend, frecv, tiles, bsend, brecv,
     lsend, lrecv, usend, urecv, dsend, drecv,
-    load_sem, o_ssem, o_rsem, f_ssem, f_rsem, h_ssem, h_rsem,
+    load_sem, o_ssem, o_rsem, f_ssem, f_rsem, h_ssem, h_rsem, w_ssem, w_rsem,
 ):
     gx, gy = lax.axis_index("gx"), lax.axis_index("gy")
     up, down = lax.rem(gx + GX - 1, GX), lax.rem(gx + 1, GX)
@@ -71,6 +72,7 @@
 
     offsets = sorted(range(1, GY), key=lambda o: -far(o))
     my_y, my_x = gy // side, lax.rem(gy, side)
+    whole, packed_to = offsets[:FAR], offsets[FAR:]
     peers = {
         o: lax.rem(my_y + o // side, side) * side + lax.rem(my_x + o % side, side) for o in offsets
     }
@@ -132,13 +134,22 @@
 
     sends = []
     o_copies = [
-        send(osend.at[peers[o]], orecv.at[gy], o_ssem.at[o], o_rsem.at[o], {"gy": peers[o]}) for o in offsets
+        send(osend.at[peers[o]], orecv.at[gy], o_ssem.at[o], o_rsem.at[o], {"gy": peers[o]}) for o in packed_to
     ]
     sends += o_copies
     orecv[gy] = osend[gy]
+    for o in whole:
+        sender = side * lax.rem(my_y + side - o // side, side) + lax.rem(my_x + side - o % side, side)
+        orecv[sender] = jnp.zeros((8, LANES), F32)
+        frecv[sender] = jnp.zeros((3, SLOTS, LANES), F32)
 
     row_of_tile = jnp.broadcast_to(dest_col * 8 + rank_col, (X, rows))
-    take = (row_of_tile == iota((X, rows), 1)).astype(F32)
+    take = [(row_of_tile == iota((X, rows), 1)).astype(F32)]
+    for o in whole:
+        sender = side * lax.rem(my_y + side - o // side, side) + lax.rem(my_x + side - o % side, side)
+        here = (dest_col == sender) & (slot_col == iota((X, X), 1))
+        take.append(here.astype(F32))
+    take = jnp.concatenate(take, axis=1)
     tiles[...] = jnp.zeros_like(tiles)
 
     c_veg.wait()
@@ -164,6 +175,12 @@
     landn[0] = skin
     landn[1] = canopy
     fields = jnp.concatenate([draw0, draw1, through], axis=1)
+    for f, part in enumerate((draw0, draw1, through)):
+        bsend[f] = part
+    w_copies = [
+        send(bsend, brecv.at[n], w_ssem.at[n], w_rsem.at[n], {"gy": peers[o]}) for n, o in enumerate(whole)
+    ]
+    sends += w_copies
 
     for ref in (rp, wp, ap, mp):
         for k in range(Z):
@@ -247,7 +264,7 @@
     for f in range(3):
         fsend[:, f, :, :] = packed[:, f * LANES:(f + 1) * LANES].reshape(GY, 8, LANES)[:, :SLOTS, :]
     f_copies = [
-        send(fsend.at[peers[o]], frecv.at[gy], f_ssem.at[o], f_rsem.at[o], {"gy": peers[o]}) for o in offsets
+        send(fsend.at[peers[o]], frecv.at[gy], f_ssem.at[o], f_rsem.at[o], {"gy": peers[o]}) for o in packed_to
     ]
     sends += f_copies
     frecv[gy] = fsend[gy]
@@ -361,11 +378,14 @@
         return d, grow, update(k, 4, d, acc), acc_g
 
     _, _, acc, acc_g = lax.fori_loop(1, Z, downward, (d, jnp.ones_like(zero), acc, zero), unroll=8)
-    for f in f_copies:
+    for f in w_copies + f_copies:
         f.wait_recv()
     for f in range(3):
         tiles[f, :, :SLOTS, :] = frecv[:, f, :, :]
-    got = pick_rows(take, jnp.concatenate([tiles[f].reshape(rows, LANES) for f in range(3)], axis=1))
+    given = [jnp.concatenate([tiles[f].reshape(rows, LANES) for f in range(3)], axis=1)]
+    for n in range(FAR):
+        given.append(jnp.concatenate([brecv[n, f] for f in range(3)], axis=1))
+    got = pick_rows(take, jnp.concatenate(given, axis=0))
     ext0 = got[:, :LANES] * s0[0]
     ext1 = got[:, LANES:2 * LANES] * s0[1]
     fall = got[:, 2 * LANES:]
@@ -547,13 +567,15 @@
             pltpu.VMEM((GY, 3, SLOTS, LANES), F32),
             pltpu.VMEM((GY, 3, SLOTS, LANES), F32),
             pltpu.VMEM((3, GY, 8, LANES), F32),
+            pltpu.VMEM((3, X, LANES), F32),
+            pltpu.VMEM((FAR, 3, X, LANES), F32),
             pltpu.VMEM((4, X, LANES), F32),
             pltpu.VMEM((4, 2, X, LANES), F32),
             pltpu.VMEM((7, Z, LANES), F32),
             pltpu.VMEM((6, Z, LANES), F32),
             pltpu.VMEM((7, Z, LANES), F32),
             pltpu.VMEM((6, Z, LANES), F32),
-            dma((9,)), dma((GY,)), dma((GY,)), dma((GY,)), dma((GY,)), dma((4, 4)), dma((4, 4)),
+            dma((9,)), dma((GY,)), dma((GY,)), dma((GY,)), dma((GY,)), dma((4, 4)), dma((4, 4)), dma((FAR,)), dma((FAR,)),
         ],
         compiler_params=pltpu.CompilerParams(
             collective_id=0, has_side_effects=True, vmem_limit_bytes=24 * 1024 * 1024

time: 28.6 us -> 28.3 us (0.990)
  Pallas kernels: 27.8 us -> 27.5 us
where the time goes in v4:
time: 28.3 us; the launch traced here: 28.2 us
  Pallas kernels  27.5 us (97%)
  between operations  0.64 us (2%)
    pallas_call x1, Pallas kernels, shards(): pl.pallas_call(functools.partial(kernel, Z, X, GX, GY), out_shape=(exact,...  26.3 us
    pallas_call x1, Pallas kernels, shards(): pl.pallas_call(functools.partial(finale, Z, X), out_shape=(f32((Z, X, LAN...  1.27 us

profile of v4, /device:TPU:2, one launch (start us, length us, event | category | flops | bytes accessed | tf_op | source)
XLA Modules:
  0.0 28.2 jit_solution(14381488016493478175)
XLA Ops:
  0.6 26.3 %shard_map.120 = (f32[32,32,128]{2,1,0:T(8,128)S(1)}, f32[2,32,128]{2,1,0:T(8,128)S(1)}, f32[1056,128]{1,0:T(8,128)S(1)}, f32[1056,128]{1,0:T(8,128)S(1)}, f32[3...) custom-call(f32[32,32,128]{2,1,0:T(8,128)} %p_hbm.1, ...), custom_call_target="tpu_custom_call" | custom-call | tf_op jit(solution)/shard_map/pallas_call | solution.py:554
  26.9 1.3 %shard_map.121 = (f32[32,32,128]{2,1,0:T(8,128)}, f32[32,32,128]{2,1,0:T(8,128)}, f32[32,32,128]{2,1,0:T(8,128)}, f32[2,32,128]{2,1,0:T(8,128)}) custom-call(f32[32,32,128]{2,1,0:T(8,128)S(1)} %get-tuple-element.13.pc, f32[2,32,128]{2,1,0:T(8,128)S(1)} %get-tuple-element.14.landn, f32[1056,128]{1,0:T(8,128)S(1)} %get-tuple-element.15.dg, ...), custom_call_target="tpu_custom_call" | custom-call | tf_op jit(solution)/shard_map/pallas_call | solution.py:584

commit v5 on v4

--- a/solution.py
+++ b/solution.py
@@ -58,6 +58,7 @@
     up, down = lax.rem(gx + GX - 1, GX), lax.rem(gx + 1, GX)
     left, right = lax.rem(gy + GY - 1, GY), lax.rem(gy + 1, GY)
     stride = X + 2 * PAD
+    mid = X // 2
     side = math.isqrt(GY)
 
     def layer(k, shift=0):
@@ -245,9 +246,10 @@
     finish(c)
 
     def halo(phase, row0, nrows):
+        part = pl.ds(0, X if phase < 2 else mid)
         cs = [
-            send(lsend.at[phase], lrecv.at[phase, 0], h_ssem.at[phase, 0], h_rsem.at[phase, 0], {"gy": right}),
-            send(lsend.at[phase], lrecv.at[phase, 1], h_ssem.at[phase, 1], h_rsem.at[phase, 1], {"gy": left}),
+            send(lsend.at[phase, part], lrecv.at[phase, 0, part], h_ssem.at[phase, 0], h_rsem.at[phase, 0], {"gy": right}),
+            send(lsend.at[phase, part], lrecv.at[phase, 1, part], h_ssem.at[phase, 1], h_rsem.at[phase, 1], {"gy": left}),
             send(usend.at[pl.ds(row0, nrows)], urecv.at[pl.ds(row0, nrows)],
                  h_ssem.at[phase, 2], h_rsem.at[phase, 2], {"gx": up}),
             send(dsend.at[pl.ds(row0, nrows)], drecv.at[pl.ds(row0, nrows)],
@@ -287,6 +289,15 @@
     h1 = halo(1, 2, 2)
 
     def lane_halo(phase):
+        if phase >= 2:
+            from_right, from_left = lrecv[phase, 1, :mid, :], lrecv[phase, 0, :mid, :]
+            return jnp.concatenate(
+                [
+                    jnp.where(even[:mid], pltpu.roll(from_right, n - 1, 1), pltpu.roll(from_left, n % LANES + 1, 1))
+                    for n in (LANES, HALF)
+                ],
+                axis=0,
+            )
         return jnp.where(
             even, pltpu.roll(lrecv[phase, 1], LANES - 1, 1), pltpu.roll(lrecv[phase, 0], 1, 1)
         )
@@ -307,10 +318,16 @@
         (urecv[1], dsend[1], below_in),
     )
 
+    def own_lanes(phase):
+        if phase < 2:
+            return lsend[phase]
+        folded = lsend[phase, :mid, :]
+        return jnp.concatenate([folded, pltpu.roll(folded, HALF, 1)], axis=0)
+
     def own_state(phase, n):
         return [
             (0.5 * root_conduct(sigmoid(op), ok), op)
-            for (_, ok, _), op in zip(edge_k, (lsend[phase], usend[n], dsend[n]))
+            for (_, ok, _), op in zip(edge_k, (own_lanes(phase), usend[n], dsend[n]))
         ]
 
     def edge_state(phase, n, own):
@@ -350,11 +367,19 @@
         gg[k + 1] = g
         return inv, b
 
+    def fold_edges(k, value, acc):
+        upper = pltpu.roll(value[:mid], 2 * k + 1, 1)
+        lower = pltpu.roll(value[mid:], HALF + 2 * k + 1, 1)
+        return jnp.where(pair[:mid] == k, upper, jnp.where(pair[:mid] == k + HALF // 2, lower, acc))
+
+    def fold(value):
+        return jnp.where(lane[:mid] < HALF, value[:mid], value[mid:])
+
     def update(k, n, d, acc):
         p = pc[k] + d
         pc[k] = p
         edge_rows(k, n, p)
-        return jnp.where(pair == k, pltpu.roll(p, 2 * k + 1, 1), acc)
+        return fold_edges(k, p, acc)
 
     lanes = side_terms(0, 0, own_state(0, 0))
     c = lax.fori_loop(0, Z - 1, lambda i, c: from_below(lanes, Z - 1 - i, c), (zero, zero), unroll=4)
@@ -362,7 +387,7 @@
     c = from_below(lanes, 0, c)
     inv0 = c[0]
     d = yy[0]
-    acc = update(0, 4, d, zero)
+    acc = update(0, 4, d, zero[:mid])
     slope[0] = zero
     usend[6, 0:1, :] = zero[0:1]
     dsend[6, 0:1, :] = zero[0:1]
@@ -374,10 +399,10 @@
         grow = jnp.where(k > 1, g * grow, grow)
         slope[k] = grow
         edge_rows(k, 6, grow)
-        acc_g = jnp.where(pair == k, pltpu.roll(grow, 2 * k + 1, 1), acc_g)
+        acc_g = fold_edges(k, grow, acc_g)
         return d, grow, update(k, 4, d, acc), acc_g
 
-    _, _, acc, acc_g = lax.fori_loop(1, Z, downward, (d, jnp.ones_like(zero), acc, zero), unroll=8)
+    _, _, acc, acc_g = lax.fori_loop(1, Z, downward, (d, jnp.ones_like(zero), acc, zero[:mid]), unroll=8)
     for f in w_copies + f_copies:
         f.wait_recv()
     for f in range(3):
@@ -401,7 +426,8 @@
             jnp.broadcast_to(value[:, :1], (X, LANES)),
         )
 
-    lsend[2] = acc + acc_g * ends(d1) + jnp.where(pair == 0, ends(d0), 0.0)
+    top = (pair[:mid] == 0) | (pair[:mid] == HALF // 2)
+    lsend[2, :mid, :] = acc + acc_g * fold(ends(d1)) + jnp.where(top, fold(ends(d0)), 0.0)
     first = iota((Z, LANES), 0) == 0
     for ref, row in ((usend, 0), (dsend, X - 1)):
         d0_row, d1_row = (jnp.broadcast_to(v[row:row + 1], (Z, LANES)) for v in (d0, d1))
@@ -429,7 +455,7 @@
     g = kvs[half] * inv_t
     d_b = (b_b + g * b_t) * inv_b / (1.0 - kvs[half] * g * inv_b)
     d_t = yy[half - 1] + g * d_b
-    acc = update(half, 5, d_b, update(half - 1, 5, d_t, zero))
+    acc = update(half, 5, d_b, update(half - 1, 5, d_t, zero[:mid]))
 
     def outward(i, c):
         d_t, d_b, acc = c
@@ -438,7 +464,7 @@
         d_b = yy[b] + gg[b] * d_b
         return d_t, d_b, update(b, 5, d_b, update(t, 5, d_t, acc))
 
-    lsend[3] = lax.fori_loop(1, half, outward, (d_t, d_b, acc), unroll=15)[2]
+    lsend[3, :mid, :] = lax.fori_loop(1, half, outward, (d_t, d_b, acc), unroll=15)[2]
     h3 = halo(3, 5, 1)
 
     def flow(t, u, u_n, m, m_n):
@@ -529,12 +555,14 @@
         vv[k] = (old * m - 0.2 * out_m) * inv + (0.4 - a2) * a2
         return 0
 
-    chunk = Z // 4
-    for n in range(4):
-        lax.fori_loop(n * chunk, (n + 1) * chunk, ages, 0, unroll=8)
-        at = pl.ds(n * chunk, chunk)
+    done = 0
+    for end in (3 * Z // 8, 3 * Z // 4, Z):
+        chunk = end - done
+        lax.fori_loop(done, done + chunk, ages, 0, unroll=chunk)
+        at = pl.ds(done, chunk)
         store(av.at[at], a_out.at[at])
         store(vv.at[at], v_out.at[at])
+        done += chunk
     for c in copies:
         c.wait()
 

time: 28.3 us -> 28.1 us (level)
  no operation moved by 1% of the time
where the time goes in v5:
time: 28.1 us; the launch traced here: 28 us
  Pallas kernels  27.4 us (98%)
  between operations  0.64 us (2%)
    pallas_call x1, Pallas kernels, shards(): pl.pallas_call(functools.partial(kernel, Z, X, GX, GY), out_shape=(exact,...  26.1 us
    pallas_call x1, Pallas kernels, shards(): pl.pallas_call(functools.partial(finale, Z, X), out_shape=(f32((Z, X, LAN...  1.27 us

profile of v5, /device:TPU:2, one launch (start us, length us, event | category | flops | bytes accessed | tf_op | source)
XLA Modules:
  0.0 28.0 jit_solution(3544215841208683029)
XLA Ops:
  0.6 26.1 %shard_map.120 = (f32[32,32,128]{2,1,0:T(8,128)S(1)}, f32[2,32,128]{2,1,0:T(8,128)S(1)}, f32[1056,128]{1,0:T(8,128)S(1)}, f32[1056,128]{1,0:T(8,128)S(1)}, f32[3...) custom-call(f32[32,32,128]{2,1,0:T(8,128)} %p_hbm.1, ...), custom_call_target="tpu_custom_call" | custom-call | tf_op jit(solution)/shard_map/pallas_call | solution.py:582
  26.7 1.3 %shard_map.121 = (f32[32,32,128]{2,1,0:T(8,128)}, f32[32,32,128]{2,1,0:T(8,128)}, f32[32,32,128]{2,1,0:T(8,128)}, f32[2,32,128]{2,1,0:T(8,128)}) custom-call(f32[32,32,128]{2,1,0:T(8,128)S(1)} %get-tuple-element.13.pc, f32[2,32,128]{2,1,0:T(8,128)S(1)} %get-tuple-element.14.landn, f32[1056,128]{1,0:T(8,128)S(1)} %get-tuple-element.15.dg, ...), custom_call_target="tpu_custom_call" | custom-call | tf_op jit(solution)/shard_map/pallas_call | solution.py:612
